TPU v7x, 32 devices: a whole 2x2x4 slice. The times are simulated.
32 devices in a mesh: half: 2 (over core), cls: 2 (over y), img: 8 (over z, x).
Axes of the slice: x: 2, y: 2, z: 4, core: 2. Of those that a mesh axis runs over, the one named last changes fastest.
Arguments:
- images: bfloat16 [2, 4096, 2, 8320], P('half', ('cls', 'img')), may hold values from -8 to 8
- projections: bfloat16 [2, 8, 8, 2, 8320], P('half', 'cls', None, None, 'img'), may hold values from -8 to 8
- ctf_table: float32 [2, 32, 8320], P('half'), may hold values from -1 to 1
- ctf_group: int32 [2, 4096], P('half', ('cls', 'img')), may hold values from 0 to 31
- orient_ids: int32 [2, 4096, 4], P('half', ('cls', 'img')), may hold values from 0 to 7
- trans_ids: int32 [2, 8], P('half'), may hold values from 0 to 24
- inv_sigma: float32 [2, 8320], P('half'), may hold values from 0.5 to 2
- counts: int32 [2, 16], P('half', ('cls', 'img')), may hold values from 1 to 256, 2560 in all within a row
Outputs:
- posterior: bfloat16 [2, 4096, 512], P('half', ('cls', 'img'))
- slab: float32 [2, 8, 8, 2, 8320], P('half', 'cls', None, None, 'img')
- fsc_map: float32 [2, 8, 8, 8320], P('half', 'cls', None, 'img')
Inputs may be any that keep to these rules, and one draw needn't show every extreme that they name: counts[h, s] is the number of live particles of shard s, held in its first slots; each half-set's counts sum to 2560, and the largest is 256.
All inputs are finite; a program needn't handle non-finite values.
Results may differ from a plain program's by a relative error of at most 0.013.
The roundings to bfloat16 on the way count: a program that leaves them out, or rounds other values in their place, can miss the bound.
Values may be sent and summed in bfloat16 or wider, within the bound.
A program may use at most 192 MiB of HBM per device.

v0:
```python
import math

import jax
import jax.numpy as jnp
from jax import lax
from jax.sharding import PartitionSpec as P

K = 8
BOX = 128
O = 8
TR = 8
TGRID = 5


def swapped(value, axis, bit):
    return lax.ppermute(value, axis, [(i, i ^ 1 << bit) for i in range(lax.axis_size(axis))])


def phases(trans_list, count):
    half_width = BOX // 2 + 1
    freq_index = jnp.arange(count, dtype=jnp.int32)
    row_index = freq_index // half_width
    col_index = freq_index % half_width
    wave_x = (row_index - BOX * (row_index >= BOX // 2).astype(jnp.int32)).astype(jnp.float32)
    wave_y = col_index.astype(jnp.float32)
    shift_x = (trans_list % TGRID - TGRID // 2).astype(jnp.float32)
    shift_y = (trans_list // TGRID - TGRID // 2).astype(jnp.float32)
    angle = (
        2.0
        * math.pi
        / BOX
        * (shift_x[:, None] * wave_x[None, :] + shift_y[:, None] * wave_y[None, :])
    )
    return (jnp.cos(angle), jnp.sin(angle))


def shift_sections(sections, inverse, cosine, sine):
    real_part = sections[:, :, 0, :].astype(jnp.float32) * inverse
    imag_part = sections[:, :, 1, :].astype(jnp.float32) * inverse
    shifted_re = real_part[:, :, None, :] * cosine - imag_part[:, :, None, :] * sine
    shifted_im = real_part[:, :, None, :] * sine + imag_part[:, :, None, :] * cosine
    return jnp.stack([shifted_re, shifted_im], axis=3).astype(jnp.bfloat16)


def section_power(sections):
    real_part = sections[:, :, 0, :].astype(jnp.float32)
    imag_part = sections[:, :, 1, :].astype(jnp.float32)
    total = real_part * real_part + imag_part * imag_part
    return total.reshape(-1, total.shape[-1])


def contract_last(left, right):
    return lax.dot_general(
        left, right, (((1,), (1,)), ((), ())), preferred_element_type=jnp.float32
    )


def contract_high(left, right):
    return lax.dot_general(
        left,
        right,
        (((1,), (1,)), ((), ())),
        precision=lax.Precision.HIGHEST,
        preferred_element_type=jnp.float32,
    )


def on_device(images, projections, ctf_table, ctf_group, orient_ids, trans_ids, inv_sigma, counts):
    num_rows = images.shape[1]
    freqs = images.shape[3]
    groups = ctf_table.shape[1]
    inverse = inv_sigma[0]
    table = ctf_table[0]
    onehot = (ctf_group[0][:, None] == jnp.arange(groups, dtype=jnp.int32)[None, :]).astype(
        jnp.float32
    )
    ctf_rows = jnp.dot(
        onehot, table, precision=lax.Precision.HIGHEST, preferred_element_type=jnp.float32
    )
    weighted = (ctf_rows[:, None, :] * images[0].astype(jnp.float32)).astype(jnp.bfloat16)
    flat_images = weighted.reshape(num_rows, 2 * freqs)
    ctf_power = table * table * inverse
    translations = trans_ids[0]
    cosine, sine = phases(translations, freqs)
    full_sections = lax.all_gather(projections[0], "img", axis=3, tiled=True)
    piece = lax.all_gather(full_sections, "cls", axis=0, tiled=True)
    number = piece.shape[0]
    shifted = shift_sections(piece, inverse, cosine, sine).reshape(number * O * TR, 2 * freqs)
    cross_terms = contract_last(flat_images, shifted)
    norm_rows = jnp.dot(
        onehot,
        contract_high(ctf_power, section_power(piece)),
        precision=lax.Precision.HIGHEST,
        preferred_element_type=jnp.float32,
    )
    block = (
        cross_terms.reshape(num_rows, number, O, TR)
        - 0.5 * norm_rows.reshape(num_rows, number, O)[:, :, :, None]
    )
    allowed = jnp.any(
        orient_ids[0][:, :, None] == jnp.arange(O, dtype=jnp.int32)[None, None, :], axis=1
    )
    mask = jnp.broadcast_to(allowed[:, None, :, None], block.shape)
    top = jnp.max(jnp.where(mask, block, -jnp.inf), axis=(1, 2, 3), keepdims=True)
    expo = jnp.exp(jnp.where(mask, block - top, -jnp.inf))
    total = jnp.sum(expo, axis=(1, 2, 3), keepdims=True)
    live = (jnp.arange(num_rows, dtype=jnp.int32) < counts[0, 0]).astype(jnp.float32)
    weights = (expo / total * live[:, None, None, None]).astype(jnp.bfloat16)
    per_class = jnp.moveaxis(weights, 1, 0).reshape(K, num_rows, O * TR)

    def back_class(class_weights):
        summed = lax.dot_general(
            class_weights, flat_images, (((0,), (0,)), ((), ())), preferred_element_type=jnp.float32
        )
        summed = summed.reshape(O, TR, 2, freqs)
        slab_re = jnp.sum(summed[:, :, 0] * cosine + summed[:, :, 1] * sine, axis=1)
        slab_im = jnp.sum(summed[:, :, 1] * cosine - summed[:, :, 0] * sine, axis=1)
        return jnp.stack([slab_re, slab_im], axis=1)

    terms = lax.map(back_class, per_class)
    owned = lax.psum_scatter(
        terms.astype(jnp.bfloat16), "cls", scatter_dimension=0, tiled=True
    ).astype(jnp.float32)
    own_slab = lax.psum_scatter(owned, "img", scatter_dimension=3, tiled=True)
    partner = swapped(own_slab.astype(jnp.bfloat16), "half", 0).astype(own_slab.dtype)
    product = own_slab[:, :, 0] * partner[:, :, 0] + own_slab[:, :, 1] * partner[:, :, 1]
    return (weights.reshape(num_rows, K * O * TR)[None], own_slab[None], product[None])


def solution(mesh):
    return jax.shard_map(
        on_device,
        mesh=mesh,
        in_specs=(
            P("half", ("cls", "img"), None, None),
            P("half", "cls", None, None, "img"),
            P("half", None, None),
            P("half", ("cls", "img")),
            P("half", ("cls", "img"), None),
            P("half", None),
            P("half", None),
            P("half", ("cls", "img")),
        ),
        out_specs=(
            P("half", ("cls", "img"), None),
            P("half", "cls", None, None, "img"),
            P("half", "cls", None, "img"),
        ),
        check_vma=False,
    )
```

profile of v0, /device:TPU:0, one launch (start us, length us, event | category | flops | bytes accessed | tf_op | source)
XLA Modules:
  0.0 719.0 jit_solution(4837378577973950024)
XLA Ops:
  7.2 4.2 copy.37
  12.2 24.1 %copy.41 = f32[1,256,2,8320]{1,3,2,0:T(8,128)} copy(bf16[1,256,2,8320]{3,2,1,0:T(2,128)(2,1)} %param.10) | data formatting | bytes 25559040 | tf_op jit(solution)/shard_map/convert_element_type | solution.py:80
  36.3 7.0 fusion.25
  43.3 9.1 %copy.56 = f32[256,8320]{0,1:T(8,128)} copy(f32[256,8320]{1,0:T(8,128)} %fusion.25) | data formatting | bytes 17039360
  52.5 25.1 %fusion.14 = bf16[256,16640]{0,1:T(8,128)(2,1)} fusion(f32[1,256,2,8320]{1,3,2,0:T(8,128)} %copy.41, f32[256,8320]{0,1:T(8,128)} %copy.56), kind=kLoop, calls=%fused_computation.20 | loop fusion | flops 8519680 | bytes 34078720 | tf_op jit(solution)/shard_map/convert_element_type | solution.py:80
  77.6 11.5 %fusion.16 = bf16[256,2,8320,1,1]{2,1,0,4,3:T(2,128)(2,1)} fusion(f32[256,8320]{1,0:T(8,128)} %fusion.25, bf16[1,256,2,8320]{3,2,1,0:T(2,128)(2,1)} %param.10), kind=kLoop, calls=%fused_computation.25 | loop fusion | flops 12779520 | bytes 25559040 | tf_op jit(solution)/shard_map/convert_element_type | solution.py:80
  89.1 253.2 %all-gather.5.cloned.1.call-done = bf16[1,4,8,2,8320]{2,1,3,0,4:T(4,128)(2,1)} async-done(((bf16[1,4,8,2,1040]{2,1,3,0,4:T(4,128)(2,1)}), bf16[1,4,8,2,8320]{2,1,3,0,4:T(4,128)(2,1)}) %all-gather.5.cloned.1.call-update) | async-done | bytes 1064976 | tf_op jit(solution)/shard_map/all_gather | solution.py:85
  342.3 19.8 %copy.38 = bf16[1,4,8,2,8320]{4,2,3,0,1:T(8,128)(2,1)} copy(bf16[1,4,8,2,8320]{2,1,3,0,4:T(4,128)(2,1)} %all-gather.5.cloned.1.call-done) | data formatting | bytes 2129920 | tf_op jit(solution)/shard_map/all_gather | solution.py:85
  363.2 32.5 %all-gather.7.cloned.1.call-done = bf16[1,8,8,2,8320]{4,2,3,0,1:T(8,128)(2,1)} async-done(((bf16[1,4,8,2,8320]{4,2,3,0,1:T(8,128)(2,1)}), bf16[1,8,8,2,8320]{4,2,3,0,1:T(8,128)(2,1)}) %all-gather.7.cloned.1.call-update) | async-done | bytes 2129936 | tf_op jit(solution)/shard_map/all_gather | solution.py:86
  395.8 4.3 fusion.21
  400.6 7.5 %subtract_convert_fusion = (bf16[8,8,8,1,8320]{4,2,3,1,0:T(8,128)(2,1)}, bf16[8,8,8,1,8320]{4,2,3,1,0:T(8,128)(2,1)}) fusion(f32[8,8320]{1,0:T(8,128)S(1)} %get-tuple-element.135, f32[8,8,8320]{2,1,0:T(8,128)S(1)} %get-tuple-element.133, f32[8,8320]{1,0:T(8,128)S(1)} %get-tuple-element.134, f32[8,8,8320]{2,1,0:T(8,128)S(1)} %get-tuple-element.132), kind=kLoop, calls=%fused_computation.24 | loop fusion | flops 34078720 | bytes 21831680 | tf_op jit(solution)/shard_map/convert.2
  408.1 10.9 %select_reduce_fusion = (f32[256]{0:T(256)S(1)}, f32[256,8,8,8,1]{0,3,4,2,1:T(8,128)S(1)}) fusion(f32[256,8,8]{0,2,1:T(8,128)S(1)} %bitcast.140, pred[256,8]{0,1:T(8,128)(4,1)S(1)} %fusion.54, bf16[8,8,8,1,8320]{4,2,3,1,0:T(8,128)(2,1)} %get-tuple-element.131, bf16[8,8,8,1,8320]{4,2,3,1,0:T(8,128)(2,1)} %get-tuple-element.130, ...), kind=kOutput, calls=%fused_computation.54 | convolution fusion | flops 4396548096 | bytes 26151936 | tf_op jit(solution)/shard_map/dot_general | solution.py:53
  419.3 77.3 %while.12 = (s32[]{:T(128)}, bf16[8,8,2,8320]{3,1,2,0:T(8,128)(2,1)S(1)}, bf16[8,256,64]{1,2,0:T(8,128)(2,1)S(1)}, bf16[256,16640]{0,1:T(8,128)(2,1)}, f32[8320]...) while((s32[]{:T(128)}, ...), condition=%wide.region_6.7_spmd.clone.clone, body=%wide.region_3.6_spmd.clone.clone.sunk | while | flops 550184960 | bytes 20067500 | solution.py:120
  419.3 6.1 fusion.67
  428.9 6.1 fusion.67
  436.1 1.5 add_reduce_fusion.2
  438.6 6.1 fusion.67
  445.7 1.5 add_reduce_fusion.2
  448.3 6.1 fusion.67
  455.4 1.5 add_reduce_fusion.2
  457.9 6.1 fusion.67
  465.1 1.5 add_reduce_fusion.2
  467.6 6.1 fusion.67
  474.7 1.5 add_reduce_fusion.2
  477.2 6.1 fusion.67
  486.9 6.1 fusion.67
  498.0 32.3 %reduce-scatter.5.cloned.1.call-done = bf16[4,8,2,8320]{3,1,2,0:T(8,128)(2,1)} async-done(((bf16[8,8,2,8320]{3,1,2,0:T(8,128)(2,1)}), bf16[4,8,2,8320]{3,1,2,0:T(8,128)(2,1)}) %reduce-scatter.5.cloned.1.call-update) | async-done | bytes 1064976 | tf_op jit(solution)/shard_map/reduce_scatter | solution.py:121
  530.3 32.1 %copy.50 = f32[4,8,2,8320]{1,2,0,3:T(2,128)} copy(bf16[4,8,2,8320]{3,1,2,0:T(8,128)(2,1)} %reduce-scatter.5.cloned.1.call-done) | data formatting | bytes 3194880
  562.4 44.5 %reshape.298 = f32[8320,64]{1,0:T(8,128)} reshape(f32[8320,4,2,8]{3,2,1,0:T(2,128)} %bitcast.133) | data formatting | bytes 4259840
  606.9 89.6 %reduce-scatter.7.cloned.1.call-done = f32[1040,64]{1,0:T(8,128)} async-done(((f32[8320,64]{1,0:T(8,128)}), f32[1040,64]{1,0:T(8,128)}) %reduce-scatter.7.cloned.1.call-update) | async-done | bytes 266256
  696.5 7.8 %reshape.299 = f32[1040,4,2,8]{3,2,1,0:T(2,128)} reshape(f32[1040,64]{1,0:T(8,128)} %reduce-scatter.7.cloned.1.call-done) | data formatting | bytes 532480
  704.3 5.5 copy.51
  (82 shorter events, 26.6 us)
Async XLA Ops:
  7.2 4.4 copy-start.4
  7.2 4.4 copy-start.5
  7.2 335.1 %all-gather.5.cloned.1.call-start = ((), (), s32[]{:S(2)}) async-start(), calls=%async_computation.3 | async-start | bytes 19169280 | tf_op jit(solution)/shard_map/all_gather | solution.py:85
  11.4 384.3 %all-gather.7.cloned.1.call-start = ((), (), s32[]{:S(2)}) async-start(), calls=%async_computation.4 | async-start | bytes 3194880 | tf_op jit(solution)/shard_map/all_gather | solution.py:86
  12.2 24.1 %copy-start.3 = (s32[1,256]{1,0:T(1,128)S(1)}, s32[1,256]{1,0:T(1,128)}, u32[]{:S(2)}) copy-start(s32[1,256]{1,0:T(1,128)} %param.13) | copy-start | bytes 3076
  43.3 9.1 %copy-start.2 = (f32[1,8320]{1,0:T(1,128)S(1)}, f32[1,8320]{1,0:T(1,128)}, u32[]{:S(2)}) copy-start(f32[1,8320]{1,0:T(1,128)} %param.16) | copy-start | bytes 99844
  362.1 168.2 %reduce-scatter.5.cloned.1.call-start = ((), (), s32[]{:S(2)}) async-start(), calls=%async_computation.2 | async-start | bytes 3194880 | tf_op jit(solution)/shard_map/reduce_scatter | solution.py:121
  395.8 4.3 copy-start.1
  496.6 1.4 copy-start
  498.0 198.6 %reduce-scatter.7.cloned.1.call-start = ((), (), s32[]{:S(2)}) async-start(), calls=%async_computation.5 | async-start | bytes 4792320
  709.8 1.9 collective-permute-start
Sparse Core Ops, SparseCore 0:
  11.5 330.7 all-gather.4
  362.2 33.4 all-gather.6
  498.1 32.1 reduce-scatter.4
  607.1 89.4 reduce-scatter.6
where the time goes:
time: 725 us; the launch traced here: 719 us
  waiting for transfers between devices  408 us (56%)
  local copies, waits for them, and re-layouts  153 us (21%)
  other arithmetic  72.2 us (10%)
  matrix products  71.2 us (10%)
  between operations  14.6 us (2%)
    all_gather x1, waiting for transfers between devices, on_device(): full_sections = lax.all_gather(projections[0], 'img', axis=3, tiled=True)  253 us
    unnamed x20, local copies, waits for them, and re-layouts  106 us
    unnamed x5, waiting for transfers between devices  89.7 us
    dot_general x8, matrix products, back_class(): lax.dot_general(class_weights, flat_images, (((0,), (0,)), ((), ())), pre...  48.9 us
    convert_element_type x2, other arithmetic, on_device(): (ctf_rows[:, None, :] * images[0].astype(jnp.float32)).astype(jnp.bfloat16)  36.6 us
    all_gather x1, waiting for transfers between devices, on_device(): piece = lax.all_gather(full_sections, 'cls', axis=0, tiled=True)  32.5 us
    reduce_scatter x1, waiting for transfers between devices, on_device(): lax.psum_scatter(terms.astype(jnp.bfloat16), 'cls', scatter_dimension=0,...  32.3 us
    convert_element_type x1, local copies, waits for them, and re-layouts, on_device(): images[0].astype(jnp.float32)  24.1 us
  transfers between devices with their start and end apart: 5, of which 4 were waited for; matrix products, arithmetic and copies ran while one was open for 11% of the time, Pallas kernels for 0%

commit v1 on v0

v1 whole, which is shorter than its diff:
```python
import functools
import math

import jax
import jax.numpy as jnp
from jax import lax
from jax.experimental import pallas as pl
from jax.experimental.pallas import tpu as pltpu
from jax.sharding import PartitionSpec as P

BOX = 128
O = 8
TGRID = 5


def phases(trans_list, count):
    half_width = BOX // 2 + 1
    freq_index = jnp.arange(count, dtype=jnp.int32)
    row_index = freq_index // half_width
    col_index = freq_index % half_width
    wave_x = (row_index - BOX * (row_index >= BOX // 2).astype(jnp.int32)).astype(jnp.float32)
    wave_y = col_index.astype(jnp.float32)
    shift_x = (trans_list % TGRID - TGRID // 2).astype(jnp.float32)
    shift_y = (trans_list // TGRID - TGRID // 2).astype(jnp.float32)
    angle = (
        2.0
        * math.pi
        / BOX
        * (shift_x[:, None] * wave_x[None, :] + shift_y[:, None] * wave_y[None, :])
    )
    return (jnp.cos(angle), jnp.sin(angle))


def flip_img(value):
    return lax.ppermute(value, "img", [(i, i ^ 1) for i in range(lax.axis_size("img"))])


def flip_cls(value):
    return lax.ppermute(value, "cls", [(i, i ^ 1) for i in range(lax.axis_size("cls"))])


def rotate_img(value, step):
    lines = lax.axis_size("img") // 2
    perm = [(i, (i // 2 + step) % lines * 2 + i % 2) for i in range(2 * lines)]
    return lax.ppermute(value, "img", perm)


def add_rounded(left, right):
    return (left.astype(jnp.float32) + right.astype(jnp.float32)).astype(jnp.bfloat16)


def expectation_kernel(
    tile,
    place_ref,
    live_ref,
    group_ref,
    orient_ref,
    wre_ref,
    wim_ref,
    near_re,
    far_re,
    near_im,
    far_im,
    table_ref,
    inverse_ref,
    cos_ref,
    sin_ref,
    post_ref,
    out_near_re,
    out_far_re,
    out_near_im,
    out_far_im,
    sec_re,
    sec_im,
    shifted,
    cross,
    norm,
    slab_re,
    slab_im,
):
    rows, freqs = wre_ref.shape
    groups = table_ref.shape[0]
    trans = cos_ref.shape[0]
    _, lines, owned, width = near_re.shape
    sections = sec_re.shape[0]
    columns = sections * trans
    my_cls, my_line, my_side = place_ref[0], place_ref[1], place_ref[2]

    def place(j):
        step = lax.rem(my_line - j // 2 + lines, lines)
        side = lax.rem(my_side + j % 2, 2)
        return side, step

    for c in range(sections // owned):
        mine = my_cls == c
        for j in range(2 * lines):
            side, step = place(j)
            to = (slice(c * owned, (c + 1) * owned), slice(j * width, (j + 1) * width))
            sec_re[to] = jnp.where(mine, near_re[side, step], far_re[side, step])
            sec_im[to] = jnp.where(mine, near_im[side, step], far_im[side, step])

    cross[...] = jnp.zeros_like(cross)
    norm[...] = jnp.zeros_like(norm)

    @pl.loop(0, freqs // tile)
    def _(i):
        at = pl.ds(pl.multiple_of(i * tile, tile), tile)
        inverse = inverse_ref[:, at]
        real = sec_re[:, at].astype(jnp.float32)
        imag = sec_im[:, at].astype(jnp.float32)
        table = table_ref[:, at]
        norm[...] += lax.dot_general(
            table * table * inverse,
            real * real + imag * imag,
            (((1,), (1,)), ((), ())),
            precision=lax.Precision.HIGHEST,
            preferred_element_type=jnp.float32,
        )
        real = real * inverse
        imag = imag * inverse
        for t in range(trans):
            cosine = cos_ref[t : t + 1, at]
            sine = sin_ref[t : t + 1, at]
            to = slice(t * sections, (t + 1) * sections)
            shifted[to, :tile] = (real * cosine - imag * sine).astype(jnp.bfloat16)
            shifted[to, tile:] = (real * sine + imag * cosine).astype(jnp.bfloat16)
        images = jnp.concatenate([wre_ref[:, at], wim_ref[:, at]], axis=1)
        cross[...] += lax.dot_general(
            images,
            shifted[...],
            (((1,), (1,)), ((), ())),
            preferred_element_type=jnp.float32,
        )

    onehot = (
        group_ref[...] == lax.broadcasted_iota(jnp.int32, (rows, groups), 1)
    ).astype(jnp.float32)
    norm_rows = jnp.dot(
        onehot,
        jnp.concatenate([norm[...]] * trans, axis=1),
        precision=lax.Precision.HIGHEST,
        preferred_element_type=jnp.float32,
    )
    scores = cross[...] - 0.5 * norm_rows
    orient = lax.broadcasted_iota(jnp.int32, (rows, columns), 1) & (O - 1)
    ids = orient_ref[...]
    mask = ids[:, 0:1] == orient
    for n in range(1, ids.shape[1]):
        mask = mask | (ids[:, n : n + 1] == orient)
    top = jnp.max(jnp.where(mask, scores, -jnp.inf), axis=1, keepdims=True)
    expo = jnp.exp(jnp.where(mask, scores - top, -jnp.inf))
    total = jnp.sum(expo, axis=1, keepdims=True)
    live = (lax.broadcasted_iota(jnp.int32, (rows, 1), 0) < live_ref[0]).astype(jnp.float32)
    weights = expo / total * live
    rounded = weights.astype(jnp.bfloat16)
    source = lax.broadcasted_iota(jnp.int32, (columns, columns), 0)
    target = lax.broadcasted_iota(jnp.int32, (columns, columns), 1)
    reorder = (source == (target & (trans - 1)) * sections + target // trans).astype(
        jnp.float32
    ).astype(jnp.bfloat16)
    post_ref[...] = jnp.dot(rounded, reorder, preferred_element_type=jnp.float32).astype(
        jnp.bfloat16
    )
    turned = weights.T.astype(jnp.bfloat16)

    @pl.loop(0, freqs // tile)
    def _(i):
        at = pl.ds(pl.multiple_of(i * tile, tile), tile)
        image_re = wre_ref[:, at]
        image_im = wim_ref[:, at]
        total_re = jnp.zeros((sections, tile), jnp.float32)
        total_im = jnp.zeros((sections, tile), jnp.float32)
        for t in range(trans):
            cosine = cos_ref[t : t + 1, at]
            sine = sin_ref[t : t + 1, at]
            part = turned[t * sections : (t + 1) * sections]
            back_re = jnp.dot(part, image_re, preferred_element_type=jnp.float32)
            back_im = jnp.dot(part, image_im, preferred_element_type=jnp.float32)
            total_re += back_re * cosine + back_im * sine
            total_im += back_im * cosine - back_re * sine
        slab_re[:, at] = total_re.astype(jnp.bfloat16)
        slab_im[:, at] = total_im.astype(jnp.bfloat16)

    for c in range(sections // owned):
        mine = my_cls == c
        for j in range(2 * lines):
            side, step = place(j)
            at = (slice(c * owned, (c + 1) * owned), slice(j * width, (j + 1) * width))
            chunk_re = slab_re[at]
            chunk_im = slab_im[at]

            @pl.when(mine)
            def _():
                out_near_re[side, step] = chunk_re
                out_near_im[side, step] = chunk_im

            @pl.when(jnp.logical_not(mine))
            def _():
                out_far_re[side, step] = chunk_re
                out_far_im[side, step] = chunk_im


def on_device(images, projections, ctf_table, ctf_group, orient_ids, trans_ids, inv_sigma, counts):
    num_rows = images.shape[1]
    freqs = images.shape[3]
    groups = ctf_table.shape[1]
    _, classes, orients, _, width = projections.shape
    owned = classes * orients
    sections = owned * lax.axis_size("cls")
    lines = lax.axis_size("img") // 2
    trans = trans_ids.shape[1]
    columns = sections * trans
    tile = max(d for d in range(128, 641, 128) if freqs % d == 0)
    cls_index = lax.axis_index("cls")
    img_index = lax.axis_index("img")

    own = projections[0].reshape(owned, 2, width).transpose(1, 0, 2)
    line = jnp.stack([own] + [rotate_img(own, s) for s in range(1, lines)], axis=1)
    near_re = jnp.stack([line[0], flip_img(line[0])])
    near_im = jnp.stack([line[1], flip_cls(line[1])])
    far_re = flip_cls(near_re)
    other_im = flip_img(near_im)
    side_near_im = jnp.stack([near_im[0], other_im[0]])
    side_far_im = jnp.stack([near_im[1], other_im[1]])

    table = ctf_table[0]
    onehot = (ctf_group[0][:, None] == jnp.arange(groups, dtype=jnp.int32)[None, :]).astype(
        jnp.float32
    )
    ctf_rows = jnp.dot(
        onehot, table, precision=lax.Precision.HIGHEST, preferred_element_type=jnp.float32
    )
    weighted_re = (ctf_rows * images[0, :, 0].astype(jnp.float32)).astype(jnp.bfloat16)
    weighted_im = (ctf_rows * images[0, :, 1].astype(jnp.float32)).astype(jnp.bfloat16)
    cosine, sine = phases(trans_ids[0], freqs)

    place = jnp.stack([cls_index, img_index // 2, img_index % 2]).astype(jnp.int32)
    chunks = jax.ShapeDtypeStruct((2, lines, owned, width), jnp.bfloat16)
    vmem = pl.BlockSpec(memory_space=pltpu.VMEM)
    smem = pl.BlockSpec(memory_space=pltpu.SMEM)
    post, out_near_re, out_far_re, out_near_im, out_far_im = pl.pallas_call(
        functools.partial(expectation_kernel, tile),
        out_shape=[
            jax.ShapeDtypeStruct((num_rows, columns), jnp.bfloat16),
            chunks,
            chunks,
            chunks,
            chunks,
        ],
        in_specs=[smem, smem] + [vmem] * 12,
        out_specs=[vmem] * 5,
        scratch_shapes=[
            pltpu.VMEM((sections, freqs), jnp.bfloat16),
            pltpu.VMEM((sections, freqs), jnp.bfloat16),
            pltpu.VMEM((columns, 2 * tile), jnp.bfloat16),
            pltpu.VMEM((num_rows, columns), jnp.float32),
            pltpu.VMEM((groups, sections), jnp.float32),
            pltpu.VMEM((sections, freqs), jnp.bfloat16),
            pltpu.VMEM((sections, freqs), jnp.bfloat16),
        ],
        compiler_params=pltpu.CompilerParams(vmem_limit_bytes=50 * 1024 * 1024),
        cost_estimate=pl.CostEstimate(
            flops=8 * num_rows * columns * freqs,
            bytes_accessed=8 * num_rows * freqs,
            transcendentals=num_rows * columns,
        ),
    )(
        place,
        counts[0],
        ctf_group[0][:, None],
        orient_ids[0],
        weighted_re,
        weighted_im,
        near_re,
        far_re,
        side_near_im,
        side_far_im,
        table,
        inv_sigma,
        cosine,
        sine,
    )

    sum_re = add_rounded(out_near_re, flip_cls(out_far_re))
    away = flip_img(jnp.stack([out_near_im[1], out_far_im[1]]))
    sum_im = add_rounded(jnp.stack([out_near_im[0], out_far_im[0]]), away)
    line_re = add_rounded(sum_re[0], flip_img(sum_re[1]))
    line_im = add_rounded(sum_im[0], flip_cls(sum_im[1]))
    lines_both = jnp.stack([line_re, line_im], axis=1)
    own_slab = lines_both[0].astype(jnp.float32)
    for s in range(1, lines):
        own_slab = own_slab + rotate_img(lines_both[s], lines - s).astype(jnp.float32)
    partner = lax.ppermute(own_slab.astype(jnp.bfloat16), "half", [(0, 1), (1, 0)]).astype(
        jnp.float32
    )
    product = own_slab[0] * partner[0] + own_slab[1] * partner[1]
    slab = own_slab.transpose(1, 0, 2).reshape(classes, orients, 2, width)
    return (post[None], slab[None], product.reshape(classes, orients, width)[None])


def solution(mesh):
    return jax.shard_map(
        on_device,
        mesh=mesh,
        in_specs=(
            P("half", ("cls", "img"), None, None),
            P("half", "cls", None, None, "img"),
            P("half", None, None),
            P("half", ("cls", "img")),
            P("half", ("cls", "img"), None),
            P("half", None),
            P("half", None),
            P("half", ("cls", "img")),
        ),
        out_specs=(
            P("half", ("cls", "img"), None),
            P("half", "cls", None, None, "img"),
            P("half", "cls", None, "img"),
        ),
        check_vma=False,
    )
```

time: 725 us -> 129 us (0.18)
  waiting for transfers between devices: 408 us -> 39.8 us
  local copies, waits for them, and re-layouts: 153 us -> 20.6 us
  other arithmetic: 72.2 us -> 5.76 us
  matrix products: 71.2 us -> 8.29 us
  Pallas kernels: 0 us -> 31.9 us
  starting transfers between devices: 0.24 us -> 20.7 us
  between operations: 14.6 us -> 1.52 us
    all_gather x2 -> x0, waiting for transfers between devices: 286 us -> none  [the longest x1 253 us: on_device(): full_sections = lax.all_gather(projections[0], 'img', axis=3, tiled=True)]
    unnamed x20 -> x15, local copies, waits for them, and re-layouts: 106 us -> 2.9 us
    unnamed x5 -> x0, waiting for transfers between devices: 89.7 us -> none
    dot_general x11 -> x0, matrix products: 64.3 us -> none  [the longest x8 48.9 us: back_class(): lax.dot_general(class_weights, flat_images, (((0,), (0,)), ((), ())), pre...]
    ppermute x1 -> x15, waiting for transfers between devices: 0.01 us -> 39.8 us  [the longest x4 26.4 us: flip_cls(): lax.ppermute(value, 'cls', [(i, i ^ 1) for i in range(lax.axis_size('cls'...]
    convert_element_type x5 -> x3, other arithmetic: 36.8 us -> 0.31 us  [the longest x2 0.29 us: add_rounded(): (left.astype(jnp.float32) + right.astype(jnp.float32)).astype(jnp.bfloat16)]
    reduce_scatter x1 -> x0, waiting for transfers between devices: 32.3 us -> none  [on_device(): lax.psum_scatter(terms.astype(jnp.bfloat16), 'cls', scatter_dimension=0,...]
    pallas_call x0 -> x1, Pallas kernels: none -> 31.9 us  [on_device(): pl.pallas_call(functools.partial(expectation_kernel, tile), out_shape=[ja...]
  transfers between devices with their start and end apart: 5 -> 15, of which waited for: 4 -> 11; matrix products, arithmetic and copies ran while one was open for 11% -> 24% of each run, Pallas kernels for 0% -> 0%
where the time goes in v1:
time: 129 us
  waiting for transfers between devices  39.8 us (31%)
  Pallas kernels  31.9 us (25%)
  starting transfers between devices  20.7 us (16%)
  local copies, waits for them, and re-layouts  20.6 us (16%)
  matrix products  8.29 us (6%)
  other arithmetic  5.76 us (4%)
  between operations  1.52 us (1%)
    pallas_call x1, Pallas kernels, on_device(): pl.pallas_call(functools.partial(expectation_kernel, tile), out_shape=[ja...  31.9 us
    ppermute x4, waiting for transfers between devices, flip_cls(): lax.ppermute(value, 'cls', [(i, i ^ 1) for i in range(lax.axis_size('cls'...  26.4 us
    slice x1, local copies, waits for them, and re-layouts, on_device(): images[0, :, 1].astype(jnp.float32)  16.6 us
    ppermute x6, starting transfers between devices, rotate_img(): return lax.ppermute(value, 'img', perm)  11.5 us
    dot_general x1, matrix products, on_device(): jnp.dot(onehot, table, precision=lax.Precision.HIGHEST, preferred_element...  8.29 us
    ppermute x4, waiting for transfers between devices, flip_img(): lax.ppermute(value, 'img', [(i, i ^ 1) for i in range(lax.axis_size('img'...  7.74 us
    ppermute x6, waiting for transfers between devices, rotate_img(): return lax.ppermute(value, 'img', perm)  5.25 us
    ppermute x4, starting transfers between devices, flip_cls(): lax.ppermute(value, 'cls', [(i, i ^ 1) for i in range(lax.axis_size('cls'...  4.81 us
  transfers between devices with their start and end apart: 15, of which 11 were waited for; matrix products, arithmetic and copies ran while one was open for 24% of the time, Pallas kernels for 0%

profile of v1, /device:TPU:0, one launch (start us, length us, event | category | flops | bytes accessed | tf_op | source)
XLA Modules:
  0.0 128.6 jit_solution(1248137355962928940)
XLA Ops:
  0.6 0.9 copy.47
  1.6 5.1 %collective-permute-start.2 = (bf16[2,32,1040]{2,1,0:T(8,128)(2,1)S(1)}, bf16[2,32,1040]{2,1,0:T(8,128)(2,1)S(1)}, u32[]{:S(2)}, u32[]{:S(2)}) collective-permute-start(bf16[2,32,1040]{2,1,0:T(8,128)(2,1)S(1)} %bitcast.108), channel_id=1, source_target_pairs={{0,6},{1,7},{2,0},{3,1},{4,2},{5,3},{6,4},{7,5},{8,14},{9,15},{10,... | collective-permute-start | bytes 399368 | tf_op jit(solution)/shard_map/ppermute | solution.py:45
  6.7 1.0 collective-permute-start
  7.7 16.6 %fusion.35 = (bf16[1,256,1,8320]{3,2,1,0:T(2,128)(2,1)S(1)}, bf16[1,256,1,8320]{3,2,1,0:T(2,128)(2,1)S(1)}) fusion(bf16[1,256,2,8320]{3,2,1,0:T(2,128)(2,1)} %param.8), kind=kLoop, calls=%fused_computation.77 | loop fusion | bytes 17039360 | tf_op jit(solution)/shard_map/slice | solution.py:234
  24.5 0.8 slice_bitcast_fusion.4
  25.3 1.5 %collective-permute-start.5 = (bf16[4,32,1040]{2,1,0:T(8,128)(2,1)S(1)}, bf16[4,32,1040]{2,1,0:T(8,128)(2,1)S(1)}, u32[]{:S(2)}, u32[]{:S(2)}) collective-permute-start(bf16[4,32,1040]{2,1,0:T(8,128)(2,1)S(1)} %get-tuple-element.34), channel_id=1, source_target_pairs={{0,8},{8,0},{1,9},{9,1},{2,10},{10,2},{3,11},{11,3},{4,12},{12,4},... | collective-permute-start | bytes 798728 | tf_op jit(solution)/shard_map/ppermute | solution.py:39
  26.8 1.0 fusion.8
  27.9 1.6 %collective-permute-start.3 = (bf16[4,32,1040]{2,1,0:T(8,128)(2,1)}, bf16[4,32,1040]{2,1,0:T(8,128)(2,1)}, u32[]{:S(2)}, u32[]{:S(2)}) collective-permute-start(bf16[4,32,1040]{2,1,0:T(8,128)(2,1)} %get-tuple-element.35), channel_id=1, source_target_pairs={{0,1},{1,0},{2,3},{3,2},{4,5},{5,4},{6,7},{7,6},{8,9},{9,8},{10,11... | collective-permute-start | bytes 798728 | tf_op jit(solution)/shard_map/ppermute | solution.py:35
  29.4 3.8 %collective-permute-done.5 = bf16[4,32,1040]{2,1,0:T(8,128)(2,1)S(1)} collective-permute-done((bf16[4,32,1040]{2,1,0:T(8,128)(2,1)S(1)}, bf16[4,32,1040]{2,1,0:T(8,128)(2,1)S(1)}, u32[]{:S(2)}, u32[]{:S(2)}) %collective-permute-start.5) | collective-permute-done | bytes 266272 | tf_op jit(solution)/shard_map/ppermute | solution.py:39
  33.2 0.9 pad_maximum_fusion
  34.2 1.5 %collective-permute-start.6 = (bf16[2,4,32,1040]{3,2,1,0:T(8,128)(2,1)}, bf16[2,4,32,1040]{3,2,1,0:T(8,128)(2,1)S(1)}, u32[]{:S(2)}, u32[]{:S(2)}) collective-permute-start(bf16[2,4,32,1040]{3,2,1,0:T(8,128)(2,1)} %pad_maximum_fusion), channel_id=1, source_target_pairs={{0,1},{1,0},{2,3},{3,2},{4,5},{5,4},{6,7},{7,6},{8,9},{9,8},{10,11... | collective-permute-start | bytes 1597448 | tf_op jit(solution)/shard_map/ppermute | solution.py:35
  35.7 8.3 %fusion = (bf16[256,8320]{1,0:T(8,128)(2,1)}, bf16[256,8320]{1,0:T(8,128)(2,1)}) fusion(bf16[1,256,1,8320]{3,2,1,0:T(2,128)(2,1)S(1)} %get-tuple-element.23, bf16[1,256,1,8320]{3,2,1,0:T(2,128)(2,1)S(1)} %get-tuple-element.24, f32[1,32,8320]{2,1,0:T(8,128)S(1)} %copy-done.1, s32[256]{0:T(256)S(1)} %bitcast.115), kind=kOutput, calls=%fused_computation.1 | convolution fusion | flops 830676992 | bytes 18105344 | tf_op jit(solution)/shard_map/dot_general | solution.py:230
  45.0 1.0 pad_maximum_fusion.3.near_re
  46.1 1.6 %collective-permute-start.4 = (bf16[2,4,32,1040]{3,2,1,0:T(8,128)(2,1)S(1)}, bf16[2,4,32,1040]{3,2,1,0:T(8,128)(2,1)S(1)}, u32[]{:S(2)}, u32[]{:S(2)}) collective-permute-start(bf16[2,4,32,1040]{3,2,1,0:T(8,128)(2,1)S(1)} %pad_maximum_fusion.3.near_re), channel_id=1, source_target_pairs={{0,8},{8,0},{1,9},{9,1},{2,10},{10,2},{3,11},{11,3},{4,12},{12,4},... | collective-permute-start | bytes 1597448 | tf_op jit(solution)/shard_map/ppermute | solution.py:39
  47.6 0.8 collective-permute-done.6
  48.5 1.2 pad_maximum_fusion.1
  49.6 9.5 %collective-permute-done.4.far_re = bf16[2,4,32,1040]{3,2,1,0:T(8,128)(2,1)S(1)} collective-permute-done((bf16[2,4,32,1040]{3,2,1,0:T(8,128)(2,1)S(1)}, bf16[2,4,32,1040]{3,2,1,0:T(8,128)(2,1)S(1)}, u32[]{:S(2)}, u32[]{:S(2)}) %collective-permute-start.4) | collective-permute-done | bytes 532512 | tf_op jit(solution)/shard_map/ppermute | solution.py:39
  59.1 0.9 copy-done.4
  60.0 31.9 %shard_map.103 = (bf16[256,512]{1,0:T(8,128)(2,1)}, bf16[2,4,32,1040]{3,2,1,0:T(8,128)(2,1)S(1)}, bf16[2,4,32,1040]{3,2,1,0:T(8,128)(2,1)S(1)}, bf16[2,4,32,1040...) custom-call(s32[3]{0:T(128)S(1)} %pad_add_fusion.place_ref, s32[1]{0:T(128)} %bitcast.102.live_ref, ...), custom_call_target="tpu_custom_call" | custom-call | flops 8724152320 | bytes 17039360 | tf_op jit(solution)/shard_map/pallas_call | solution.py:241
  91.9 1.6 %collective-permute-start.7 = (bf16[2,4,32,1040]{3,2,1,0:T(8,128)(2,1)S(1)}, bf16[2,4,32,1040]{3,2,1,0:T(8,128)(2,1)S(1)}, u32[]{:S(2)}, u32[]{:S(2)}) collective-permute-start(bf16[2,4,32,1040]{3,2,1,0:T(8,128)(2,1)S(1)} %get-tuple-element.10), channel_id=1, source_target_pairs={{0,8},{8,0},{1,9},{9,1},{2,10},{10,2},{3,11},{11,3},{4,12},{12,4},... | collective-permute-start | bytes 1597448 | tf_op jit(solution)/shard_map/ppermute | solution.py:39
  94.3 9.7 %collective-permute-done.7 = bf16[2,4,32,1040]{3,2,1,0:T(8,128)(2,1)S(1)} collective-permute-done((bf16[2,4,32,1040]{3,2,1,0:T(8,128)(2,1)S(1)}, bf16[2,4,32,1040]{3,2,1,0:T(8,128)(2,1)S(1)}, u32[]{:S(2)}, u32[]{:S(2)}) %collective-permute-start.7) | collective-permute-done | bytes 532512 | tf_op jit(solution)/shard_map/ppermute | solution.py:39
  104.2 0.6 collective-permute-start.8
  104.8 3.7 %collective-permute-done.9 = bf16[2,4,32,1040]{3,2,1,0:T(8,128)(2,1)S(1)} collective-permute-done((bf16[2,4,32,1040]{3,2,1,0:T(8,128)(2,1)S(1)}, bf16[2,4,32,1040]{3,2,1,0:T(8,128)(2,1)S(1)}, u32[]{:S(2)}, u32[]{:S(2)}) %collective-permute-start.9) | collective-permute-done | bytes 532512 | tf_op jit(solution)/shard_map/ppermute | solution.py:35
  108.8 3.2 %collective-permute-done.8 = bf16[4,32,1040]{2,1,0:T(8,128)(2,1)S(1)} collective-permute-done((bf16[4,32,1040]{2,1,0:T(8,128)(2,1)S(1)}, bf16[4,32,1040]{2,1,0:T(8,128)(2,1)S(1)}, u32[]{:S(2)}, u32[]{:S(2)}) %collective-permute-start.8) | collective-permute-done | bytes 266272 | tf_op jit(solution)/shard_map/ppermute | solution.py:35
  112.1 3.4 %collective-permute-done.10 = bf16[4,32,1040]{2,1,0:T(8,128)(2,1)S(1)} collective-permute-done((bf16[4,32,1040]{2,1,0:T(8,128)(2,1)S(1)}, bf16[4,32,1040]{2,1,0:T(8,128)(2,1)S(1)}, u32[]{:S(2)}, u32[]{:S(2)}) %collective-permute-start.10) | collective-permute-done | bytes 266272 | tf_op jit(solution)/shard_map/ppermute | solution.py:39
  115.6 2.6 %collective-permute-start.13 = (bf16[2,32,1040]{2,1,0:T(8,128)(2,1)S(1)}, bf16[2,32,1040]{2,1,0:T(8,128)(2,1)S(1)}, u32[]{:S(2)}, u32[]{:S(2)}) collective-permute-start(bf16[2,32,1040]{2,1,0:T(8,128)(2,1)S(1)} %get-tuple-element.26), channel_id=1, source_target_pairs={{0,2},{1,3},{2,4},{3,5},{4,6},{5,7},{6,0},{7,1},{8,10},{9,11},{10,... | collective-permute-start | bytes 399368 | tf_op jit(solution)/shard_map/ppermute | solution.py:45
  118.2 1.4 %collective-permute-start.12 = (bf16[2,32,1040]{2,1,0:T(8,128)(2,1)S(1)}, bf16[2,32,1040]{2,1,0:T(8,128)(2,1)S(1)}, u32[]{:S(2)}, u32[]{:S(2)}) collective-permute-start(bf16[2,32,1040]{2,1,0:T(8,128)(2,1)S(1)} %get-tuple-element.27), channel_id=1, source_target_pairs={{0,4},{1,5},{2,6},{3,7},{4,0},{5,1},{6,2},{7,3},{8,12},{9,13},{10,... | collective-permute-start | bytes 399368 | tf_op jit(solution)/shard_map/ppermute | solution.py:45
  119.6 1.4 %collective-permute-start.11 = (bf16[2,32,1040]{2,1,0:T(8,128)(2,1)S(1)}, bf16[2,32,1040]{2,1,0:T(8,128)(2,1)S(1)}, u32[]{:S(2)}, u32[]{:S(2)}) collective-permute-start(bf16[2,32,1040]{2,1,0:T(8,128)(2,1)S(1)} %get-tuple-element.25), channel_id=1, source_target_pairs={{0,6},{1,7},{2,0},{3,1},{4,2},{5,3},{6,4},{7,5},{8,14},{9,15},{10,... | collective-permute-start | bytes 399368 | tf_op jit(solution)/shard_map/ppermute | solution.py:45
  121.1 1.6 %collective-permute-done.13 = bf16[2,32,1040]{2,1,0:T(8,128)(2,1)S(1)} collective-permute-done((bf16[2,32,1040]{2,1,0:T(8,128)(2,1)S(1)}, bf16[2,32,1040]{2,1,0:T(8,128)(2,1)S(1)}, u32[]{:S(2)}, u32[]{:S(2)}) %collective-permute-start.13) | collective-permute-done | bytes 133152 | tf_op jit(solution)/shard_map/ppermute | solution.py:45
  122.6 3.3 %collective-permute-done.12 = bf16[2,32,1040]{2,1,0:T(8,128)(2,1)S(1)} collective-permute-done((bf16[2,32,1040]{2,1,0:T(8,128)(2,1)S(1)}, bf16[2,32,1040]{2,1,0:T(8,128)(2,1)S(1)}, u32[]{:S(2)}, u32[]{:S(2)}) %collective-permute-start.12) | collective-permute-done | bytes 133152 | tf_op jit(solution)/shard_map/ppermute | solution.py:45
  126.5 0.9 copy.33
  127.9 0.7 fusion.17
  (40 shorter events, 3.0 us)
Async XLA Ops:
  1.6 22.8 %collective-permute-start.2 = (bf16[2,32,1040]{2,1,0:T(8,128)(2,1)S(1)}, bf16[2,32,1040]{2,1,0:T(8,128)(2,1)S(1)}, u32[]{:S(2)}, u32[]{:S(2)}) collective-permute-start(bf16[2,32,1040]{2,1,0:T(8,128)(2,1)S(1)} %bitcast.108), channel_id=1, source_target_pairs={{0,6},{1,7},{2,0},{3,1},{4,2},{5,3},{6,4},{7,5},{8,14},{9,15},{10,... | collective-permute-start | bytes 399368 | tf_op jit(solution)/shard_map/ppermute | solution.py:45
  6.7 17.7 %collective-permute-start.1 = (bf16[2,32,1040]{2,1,0:T(8,128)(2,1)S(1)}, bf16[2,32,1040]{2,1,0:T(8,128)(2,1)S(1)}, u32[]{:S(2)}, u32[]{:S(2)}) collective-permute-start(bf16[2,32,1040]{2,1,0:T(8,128)(2,1)S(1)} %bitcast.109), channel_id=1, source_target_pairs={{0,4},{1,5},{2,6},{3,7},{4,0},{5,1},{6,2},{7,3},{8,12},{9,13},{10,... | collective-permute-start | bytes 399368 | tf_op jit(solution)/shard_map/ppermute | solution.py:45
  6.7 17.7 %collective-permute-start = (bf16[2,32,1040]{2,1,0:T(8,128)(2,1)S(1)}, bf16[2,32,1040]{2,1,0:T(8,128)(2,1)S(1)}, u32[]{:S(2)}, u32[]{:S(2)}) collective-permute-start(bf16[2,32,1040]{2,1,0:T(8,128)(2,1)S(1)} %bitcast.110), channel_id=1, source_target_pairs={{0,2},{1,3},{2,4},{3,5},{4,6},{5,7},{6,0},{7,1},{8,10},{9,11},{10,... | collective-permute-start | bytes 399368 | tf_op jit(solution)/shard_map/ppermute | solution.py:45
  7.7 16.6 %copy-start.5 = (s32[1,8]{1,0:T(1,128)S(1)}, s32[1,8]{1,0:T(1,128)}, u32[]{:S(2)}) copy-start(s32[1,8]{1,0:T(1,128)} %param.13) | copy-start | bytes 100
  24.3 11.3 %copy-start.1 = (f32[1,32,8320]{2,1,0:T(8,128)S(1)}, f32[1,32,8320]{2,1,0:T(8,128)}, u32[]{:S(2)}) copy-start(f32[1,32,8320]{2,1,0:T(8,128)} %param.10) | copy-start | bytes 3194884
  24.4 11.3 %copy-start.3 = (s32[1,256]{1,0:T(1,128)S(1)}, s32[1,256]{1,0:T(1,128)}, u32[]{:S(2)}) copy-start(s32[1,256]{1,0:T(1,128)} %param.11) | copy-start | bytes 3076
  25.3 7.9 %collective-permute-start.5 = (bf16[4,32,1040]{2,1,0:T(8,128)(2,1)S(1)}, bf16[4,32,1040]{2,1,0:T(8,128)(2,1)S(1)}, u32[]{:S(2)}, u32[]{:S(2)}) collective-permute-start(bf16[4,32,1040]{2,1,0:T(8,128)(2,1)S(1)} %get-tuple-element.34), channel_id=1, source_target_pairs={{0,8},{8,0},{1,9},{9,1},{2,10},{10,2},{3,11},{11,3},{4,12},{12,4},... | collective-permute-start | bytes 798728 | tf_op jit(solution)/shard_map/ppermute | solution.py:39
  27.9 17.1 %collective-permute-start.3 = (bf16[4,32,1040]{2,1,0:T(8,128)(2,1)}, bf16[4,32,1040]{2,1,0:T(8,128)(2,1)}, u32[]{:S(2)}, u32[]{:S(2)}) collective-permute-start(bf16[4,32,1040]{2,1,0:T(8,128)(2,1)} %get-tuple-element.35), channel_id=1, source_target_pairs={{0,1},{1,0},{2,3},{3,2},{4,5},{5,4},{6,7},{7,6},{8,9},{9,8},{10,11... | collective-permute-start | bytes 798728 | tf_op jit(solution)/shard_map/ppermute | solution.py:35
  34.2 14.2 %collective-permute-start.6 = (bf16[2,4,32,1040]{3,2,1,0:T(8,128)(2,1)}, bf16[2,4,32,1040]{3,2,1,0:T(8,128)(2,1)S(1)}, u32[]{:S(2)}, u32[]{:S(2)}) collective-permute-start(bf16[2,4,32,1040]{3,2,1,0:T(8,128)(2,1)} %pad_maximum_fusion), channel_id=1, source_target_pairs={{0,1},{1,0},{2,3},{3,2},{4,5},{5,4},{6,7},{7,6},{8,9},{9,8},{10,11... | collective-permute-start | bytes 1597448 | tf_op jit(solution)/shard_map/ppermute | solution.py:35
  35.7 9.1 %copy-start.2 = (s32[1,256,4]{1,2,0:T(4,128)S(1)}, s32[1,256,4]{1,2,0:T(4,128)}, u32[]{:S(2)}) copy-start(s32[1,256,4]{1,2,0:T(4,128)} %param.12) | copy-start | bytes 12292
  44.0 16.0 %copy-start = (f32[1,8320]{1,0:T(1,128)S(1)}, f32[1,8320]{1,0:T(1,128)}, u32[]{:S(2)}) copy-start(f32[1,8320]{1,0:T(1,128)} %inverse_ref.1) | copy-start | bytes 99844
  46.1 13.1 %collective-permute-start.4 = (bf16[2,4,32,1040]{3,2,1,0:T(8,128)(2,1)S(1)}, bf16[2,4,32,1040]{3,2,1,0:T(8,128)(2,1)S(1)}, u32[]{:S(2)}, u32[]{:S(2)}) collective-permute-start(bf16[2,4,32,1040]{3,2,1,0:T(8,128)(2,1)S(1)} %pad_maximum_fusion.3.near_re), channel_id=1, source_target_pairs={{0,8},{8,0},{1,9},{9,1},{2,10},{10,2},{3,11},{11,3},{4,12},{12,4},... | collective-permute-start | bytes 1597448 | tf_op jit(solution)/shard_map/ppermute | solution.py:39
  59.1 0.9 copy-start.4
  91.9 12.1 %collective-permute-start.7 = (bf16[2,4,32,1040]{3,2,1,0:T(8,128)(2,1)S(1)}, bf16[2,4,32,1040]{3,2,1,0:T(8,128)(2,1)S(1)}, u32[]{:S(2)}, u32[]{:S(2)}) collective-permute-start(bf16[2,4,32,1040]{3,2,1,0:T(8,128)(2,1)S(1)} %get-tuple-element.10), channel_id=1, source_target_pairs={{0,8},{8,0},{1,9},{9,1},{2,10},{10,2},{3,11},{11,3},{4,12},{12,4},... | collective-permute-start | bytes 1597448 | tf_op jit(solution)/shard_map/ppermute | solution.py:39
  93.7 14.8 %collective-permute-start.9 = (bf16[2,4,32,1040]{3,2,1,0:T(8,128)(2,1)S(1)}, bf16[2,4,32,1040]{3,2,1,0:T(8,128)(2,1)S(1)}, u32[]{:S(2)}, u32[]{:S(2)}) collective-permute-start(bf16[2,4,32,1040]{3,2,1,0:T(8,128)(2,1)S(1)} %pad_maximum_fusion.5), channel_id=1, source_target_pairs={{0,1},{1,0},{2,3},{3,2},{4,5},{5,4},{6,7},{7,6},{8,9},{9,8},{10,11... | collective-permute-start | bytes 1597448 | tf_op jit(solution)/shard_map/ppermute | solution.py:35
  104.2 7.8 %collective-permute-start.8 = (bf16[4,32,1040]{2,1,0:T(8,128)(2,1)S(1)}, bf16[4,32,1040]{2,1,0:T(8,128)(2,1)S(1)}, u32[]{:S(2)}, u32[]{:S(2)}) collective-permute-start(bf16[4,32,1040]{2,1,0:T(8,128)(2,1)S(1)} %slice_bitcast_fusion.2), channel_id=1, source_target_pairs={{0,1},{1,0},{2,3},{3,2},{4,5},{5,4},{6,7},{7,6},{8,9},{9,8},{10,11... | collective-permute-start | bytes 798728 | tf_op jit(solution)/shard_map/ppermute | solution.py:35
  108.7 6.8 %collective-permute-start.10 = (bf16[4,32,1040]{2,1,0:T(8,128)(2,1)S(1)}, bf16[4,32,1040]{2,1,0:T(8,128)(2,1)S(1)}, u32[]{:S(2)}, u32[]{:S(2)}) collective-permute-start(bf16[4,32,1040]{2,1,0:T(8,128)(2,1)S(1)} %slice_bitcast_fusion), channel_id=1, source_target_pairs={{0,8},{8,0},{1,9},{9,1},{2,10},{10,2},{3,11},{11,3},{4,12},{12,4},... | collective-permute-start | bytes 798728 | tf_op jit(solution)/shard_map/ppermute | solution.py:39
  115.6 7.0 %collective-permute-start.13 = (bf16[2,32,1040]{2,1,0:T(8,128)(2,1)S(1)}, bf16[2,32,1040]{2,1,0:T(8,128)(2,1)S(1)}, u32[]{:S(2)}, u32[]{:S(2)}) collective-permute-start(bf16[2,32,1040]{2,1,0:T(8,128)(2,1)S(1)} %get-tuple-element.26), channel_id=1, source_target_pairs={{0,2},{1,3},{2,4},{3,5},{4,6},{5,7},{6,0},{7,1},{8,10},{9,11},{10,... | collective-permute-start | bytes 399368 | tf_op jit(solution)/shard_map/ppermute | solution.py:45
  118.2 7.7 %collective-permute-start.12 = (bf16[2,32,1040]{2,1,0:T(8,128)(2,1)S(1)}, bf16[2,32,1040]{2,1,0:T(8,128)(2,1)S(1)}, u32[]{:S(2)}, u32[]{:S(2)}) collective-permute-start(bf16[2,32,1040]{2,1,0:T(8,128)(2,1)S(1)} %get-tuple-element.27), channel_id=1, source_target_pairs={{0,4},{1,5},{2,6},{3,7},{4,0},{5,1},{6,2},{7,3},{8,12},{9,13},{10,... | collective-permute-start | bytes 399368 | tf_op jit(solution)/shard_map/ppermute | solution.py:45
  119.6 6.7 %collective-permute-start.11 = (bf16[2,32,1040]{2,1,0:T(8,128)(2,1)S(1)}, bf16[2,32,1040]{2,1,0:T(8,128)(2,1)S(1)}, u32[]{:S(2)}, u32[]{:S(2)}) collective-permute-start(bf16[2,32,1040]{2,1,0:T(8,128)(2,1)S(1)} %get-tuple-element.25), channel_id=1, source_target_pairs={{0,6},{1,7},{2,0},{3,1},{4,2},{5,3},{6,4},{7,5},{8,14},{9,15},{10,... | collective-permute-start | bytes 399368 | tf_op jit(solution)/shard_map/ppermute | solution.py:45
  126.4 1.4 %collective-permute-start.14 = (bf16[2,32,1040]{2,1,0:T(8,128)(2,1)S(1)}, bf16[2,32,1040]{2,1,0:T(8,128)(2,1)S(1)}, u32[]{:S(2)}, u32[]{:S(2)}) collective-permute-start(bf16[2,32,1040]{2,1,0:T(8,128)(2,1)S(1)} %get-tuple-element.19), channel_id=1, source_target_pairs={{0,16},{16,0},{1,17},{17,1},{2,18},{18,2},{3,19},{19,3},{4,20},{20... | collective-permute-start | bytes 399368 | tf_op jit(solution)/shard_map/ppermute | solution.py:293

commit v2 on v1

--- a/solution.py
+++ b/solution.py
@@ -49,6 +49,10 @@
     return (left.astype(jnp.float32) + right.astype(jnp.float32)).astype(jnp.bfloat16)
 
 
+def place(j, my_line, my_side, lines):
+    return lax.rem(my_side + j % 2, 2), lax.rem(my_line - j // 2 + lines, lines)
+
+
 def expectation_kernel(
     tile,
     place_ref,
@@ -57,47 +61,29 @@
     orient_ref,
     wre_ref,
     wim_ref,
-    near_re,
-    far_re,
-    near_im,
-    far_im,
-    table_ref,
-    inverse_ref,
-    cos_ref,
-    sin_ref,
-    post_ref,
-    out_near_re,
-    out_far_re,
-    out_near_im,
-    out_far_im,
-    sec_re,
-    sec_im,
-    shifted,
-    cross,
-    norm,
-    slab_re,
-    slab_im,
+    *refs,
 ):
-    rows, freqs = wre_ref.shape
+    blocks_re, blocks_im = refs[:4], refs[4:8]
+    table_ref, inverse_ref, cos_ref, sin_ref, post_ref, turned_ref = refs[8:14]
+    sec_re, sec_im, shifted, cross, norm = refs[14:]
+    freqs = wre_ref.shape[1]
+    rows = group_ref.shape[0]
     groups = table_ref.shape[0]
     trans = cos_ref.shape[0]
-    _, lines, owned, width = near_re.shape
+    lines, owned, width = blocks_re[0].shape
     sections = sec_re.shape[0]
     columns = sections * trans
     my_cls, my_line, my_side = place_ref[0], place_ref[1], place_ref[2]
 
-    def place(j):
-        step = lax.rem(my_line - j // 2 + lines, lines)
-        side = lax.rem(my_side + j % 2, 2)
-        return side, step
-
     for c in range(sections // owned):
         mine = my_cls == c
         for j in range(2 * lines):
-            side, step = place(j)
+            side, step = place(j, my_line, my_side, lines)
             to = (slice(c * owned, (c + 1) * owned), slice(j * width, (j + 1) * width))
-            sec_re[to] = jnp.where(mine, near_re[side, step], far_re[side, step])
-            sec_im[to] = jnp.where(mine, near_im[side, step], far_im[side, step])
+            for section, blocks in ((sec_re, blocks_re), (sec_im, blocks_im)):
+                near = jnp.where(side == 0, blocks[0][step], blocks[1][step])
+                far = jnp.where(side == 0, blocks[2][step], blocks[3][step])
+                section[to] = jnp.where(mine, near, far)
 
     cross[...] = jnp.zeros_like(cross)
     norm[...] = jnp.zeros_like(norm)
@@ -161,43 +147,70 @@
     post_ref[...] = jnp.dot(rounded, reorder, preferred_element_type=jnp.float32).astype(
         jnp.bfloat16
     )
-    turned = weights.T.astype(jnp.bfloat16)
+    turned_ref[...] = weights.T.astype(jnp.bfloat16)
+
+
+def projection_kernel(
+    tile,
+    place_ref,
+    turned_ref,
+    wre_ref,
+    wim_ref,
+    cos_ref,
+    sin_ref,
+    out_re_same,
+    out_re_other,
+    out_im_same,
+    out_im_other,
+    slab_re,
+    slab_im,
+):
+    freqs = wre_ref.shape[1]
+    trans = cos_ref.shape[0]
+    lines, owned, width = out_re_same.shape
+    sections = turned_ref.shape[0] // trans
+    my_line, my_side, chosen = place_ref[1], place_ref[2], place_ref[3]
+    weights = jnp.concatenate(
+        [
+            turned_ref[pl.ds(pl.multiple_of(t * sections + chosen * owned, owned), owned)]
+            for t in range(trans)
+        ],
+        axis=0,
+    )
 
     @pl.loop(0, freqs // tile)
     def _(i):
         at = pl.ds(pl.multiple_of(i * tile, tile), tile)
         image_re = wre_ref[:, at]
         image_im = wim_ref[:, at]
-        total_re = jnp.zeros((sections, tile), jnp.float32)
-        total_im = jnp.zeros((sections, tile), jnp.float32)
+        back_re = jnp.dot(weights, image_re, preferred_element_type=jnp.float32)
+        back_im = jnp.dot(weights, image_im, preferred_element_type=jnp.float32)
+        total_re = jnp.zeros((owned, tile), jnp.float32)
+        total_im = jnp.zeros((owned, tile), jnp.float32)
         for t in range(trans):
             cosine = cos_ref[t : t + 1, at]
             sine = sin_ref[t : t + 1, at]
-            part = turned[t * sections : (t + 1) * sections]
-            back_re = jnp.dot(part, image_re, preferred_element_type=jnp.float32)
-            back_im = jnp.dot(part, image_im, preferred_element_type=jnp.float32)
-            total_re += back_re * cosine + back_im * sine
-            total_im += back_im * cosine - back_re * sine
+            part_re = back_re[t * owned : (t + 1) * owned]
+            part_im = back_im[t * owned : (t + 1) * owned]
+            total_re += part_re * cosine + part_im * sine
+            total_im += part_im * cosine - part_re * sine
         slab_re[:, at] = total_re.astype(jnp.bfloat16)
         slab_im[:, at] = total_im.astype(jnp.bfloat16)
 
-    for c in range(sections // owned):
-        mine = my_cls == c
-        for j in range(2 * lines):
-            side, step = place(j)
-            at = (slice(c * owned, (c + 1) * owned), slice(j * width, (j + 1) * width))
-            chunk_re = slab_re[at]
-            chunk_im = slab_im[at]
-
-            @pl.when(mine)
-            def _():
-                out_near_re[side, step] = chunk_re
-                out_near_im[side, step] = chunk_im
-
-            @pl.when(jnp.logical_not(mine))
-            def _():
-                out_far_re[side, step] = chunk_re
-                out_far_im[side, step] = chunk_im
+    for j in range(2 * lines):
+        side, step = place(j, my_line, my_side, lines)
+        chunk_re = slab_re[:, j * width : (j + 1) * width]
+        chunk_im = slab_im[:, j * width : (j + 1) * width]
+
+        @pl.when(side == 0)
+        def _():
+            out_re_same[step] = chunk_re
+            out_im_same[step] = chunk_im
+
+        @pl.when(side != 0)
+        def _():
+            out_re_other[step] = chunk_re
+            out_im_other[step] = chunk_im
 
 
 def on_device(images, projections, ctf_table, ctf_group, orient_ids, trans_ids, inv_sigma, counts):
@@ -216,76 +229,91 @@
 
     own = projections[0].reshape(owned, 2, width).transpose(1, 0, 2)
     line = jnp.stack([own] + [rotate_img(own, s) for s in range(1, lines)], axis=1)
-    near_re = jnp.stack([line[0], flip_img(line[0])])
-    near_im = jnp.stack([line[1], flip_cls(line[1])])
-    far_re = flip_cls(near_re)
-    other_im = flip_img(near_im)
-    side_near_im = jnp.stack([near_im[0], other_im[0]])
-    side_far_im = jnp.stack([near_im[1], other_im[1]])
-
-    table = ctf_table[0]
+    same_re, same_im = line[0], line[1]
+    side_re = flip_img(same_re)
+    far_im = flip_cls(same_im)
+    far_re = flip_cls(same_re)
+    side_im = flip_img(same_im)
+    table, side_re, far_im = lax.optimization_barrier((ctf_table[0], side_re, far_im))
+    blocks = [same_re, side_re, far_re, flip_cls(side_re)]
+    blocks += [same_im, side_im, far_im, flip_img(far_im)]
     onehot = (ctf_group[0][:, None] == jnp.arange(groups, dtype=jnp.int32)[None, :]).astype(
         jnp.float32
     )
     ctf_rows = jnp.dot(
         onehot, table, precision=lax.Precision.HIGHEST, preferred_element_type=jnp.float32
     )
-    weighted_re = (ctf_rows * images[0, :, 0].astype(jnp.float32)).astype(jnp.bfloat16)
-    weighted_im = (ctf_rows * images[0, :, 1].astype(jnp.float32)).astype(jnp.bfloat16)
+    weighted = [
+        (ctf_rows * images[0, :, part].astype(jnp.float32)).astype(jnp.bfloat16)
+        for part in range(2)
+    ]
     cosine, sine = phases(trans_ids[0], freqs)
 
-    place = jnp.stack([cls_index, img_index // 2, img_index % 2]).astype(jnp.int32)
-    chunks = jax.ShapeDtypeStruct((2, lines, owned, width), jnp.bfloat16)
+    place_mine = [cls_index, img_index // 2, img_index % 2]
     vmem = pl.BlockSpec(memory_space=pltpu.VMEM)
     smem = pl.BlockSpec(memory_space=pltpu.SMEM)
-    post, out_near_re, out_far_re, out_near_im, out_far_im = pl.pallas_call(
+    post, turned = pl.pallas_call(
         functools.partial(expectation_kernel, tile),
         out_shape=[
             jax.ShapeDtypeStruct((num_rows, columns), jnp.bfloat16),
-            chunks,
-            chunks,
-            chunks,
-            chunks,
+            jax.ShapeDtypeStruct((columns, num_rows), jnp.bfloat16),
         ],
-        in_specs=[smem, smem] + [vmem] * 12,
-        out_specs=[vmem] * 5,
+        in_specs=[smem, smem] + [vmem] * 16,
+        out_specs=[vmem] * 2,
         scratch_shapes=[
             pltpu.VMEM((sections, freqs), jnp.bfloat16),
             pltpu.VMEM((sections, freqs), jnp.bfloat16),
             pltpu.VMEM((columns, 2 * tile), jnp.bfloat16),
             pltpu.VMEM((num_rows, columns), jnp.float32),
             pltpu.VMEM((groups, sections), jnp.float32),
-            pltpu.VMEM((sections, freqs), jnp.bfloat16),
-            pltpu.VMEM((sections, freqs), jnp.bfloat16),
         ],
-        compiler_params=pltpu.CompilerParams(vmem_limit_bytes=50 * 1024 * 1024),
+        compiler_params=pltpu.CompilerParams(vmem_limit_bytes=40 * 1024 * 1024),
         cost_estimate=pl.CostEstimate(
-            flops=8 * num_rows * columns * freqs,
-            bytes_accessed=8 * num_rows * freqs,
+            flops=4 * num_rows * columns * freqs,
+            bytes_accessed=4 * num_rows * freqs,
             transcendentals=num_rows * columns,
         ),
     )(
-        place,
+        jnp.stack(place_mine).astype(jnp.int32),
         counts[0],
         ctf_group[0][:, None],
         orient_ids[0],
-        weighted_re,
-        weighted_im,
-        near_re,
-        far_re,
-        side_near_im,
-        side_far_im,
+        *weighted,
+        *blocks,
         table,
         inv_sigma,
         cosine,
         sine,
     )
 
-    sum_re = add_rounded(out_near_re, flip_cls(out_far_re))
-    away = flip_img(jnp.stack([out_near_im[1], out_far_im[1]]))
-    sum_im = add_rounded(jnp.stack([out_near_im[0], out_far_im[0]]), away)
-    line_re = add_rounded(sum_re[0], flip_img(sum_re[1]))
-    line_im = add_rounded(sum_im[0], flip_cls(sum_im[1]))
+    def project(chosen):
+        chunks = jax.ShapeDtypeStruct((lines, owned, width), jnp.bfloat16)
+        return pl.pallas_call(
+            functools.partial(projection_kernel, tile),
+            out_shape=[chunks] * 4,
+            in_specs=[smem] + [vmem] * 5,
+            out_specs=[vmem] * 4,
+            scratch_shapes=[
+                pltpu.VMEM((owned, freqs), jnp.bfloat16),
+                pltpu.VMEM((owned, freqs), jnp.bfloat16),
+            ],
+            compiler_params=pltpu.CompilerParams(vmem_limit_bytes=40 * 1024 * 1024),
+            cost_estimate=pl.CostEstimate(
+                flops=num_rows * columns * freqs // 8,
+                bytes_accessed=4 * num_rows * freqs,
+                transcendentals=0,
+            ),
+        )(jnp.stack(place_mine + [chosen]).astype(jnp.int32), turned, *weighted, cosine, sine)
+
+    far_re_same, far_re_other, far_im_same, far_im_other = project(1 - cls_index)
+    near_re_same, near_re_other, near_im_same, near_im_other = project(cls_index)
+
+    other_re = add_rounded(near_re_other, flip_cls(far_re_other))
+    sum_im_far = add_rounded(far_im_same, flip_img(far_im_other))
+    same_sum = add_rounded(near_re_same, flip_cls(far_re_same))
+    sum_im_near = add_rounded(near_im_same, flip_img(near_im_other))
+    line_re = add_rounded(same_sum, flip_img(other_re))
+    line_im = add_rounded(sum_im_near, flip_cls(sum_im_far))
     lines_both = jnp.stack([line_re, line_im], axis=1)
     own_slab = lines_both[0].astype(jnp.float32)
     for s in range(1, lines):

time: 129 us -> 111 us (0.86)
  waiting for transfers between devices: 39.8 us -> 27.1 us
  Pallas kernels: 31.9 us -> 27.8 us
  other arithmetic: 5.76 us -> 2.67 us
  matrix products: 8.29 us -> 10.6 us
    pallas_call x1, Pallas kernels: 31.9 us -> 13.4 us  [on_device(): pl.pallas_call(functools.partial(expectation_kernel, tile), out_shape=[ja...]
    pallas_call x0 -> x2, Pallas kernels: none -> 14.4 us  [project(): pl.pallas_call(functools.partial(projection_kernel, tile), out_shape=[chu...]
    ppermute x4 -> x6, waiting for transfers between devices: 26.4 us -> 13.9 us  [flip_cls(): lax.ppermute(value, 'cls', [(i, i ^ 1) for i in range(lax.axis_size('cls'...]
    another operation x5 -> x3, other arithmetic: 3.31 us -> 0.23 us  [the longest x2 0.16 us: project(): jnp.stack(place_mine + [chosen]).astype(jnp.int32)]
    ppermute x4 -> x6, waiting for transfers between devices: 7.74 us -> 5.14 us  [flip_img(): lax.ppermute(value, 'img', [(i, i ^ 1) for i in range(lax.axis_size('img'...]
    ppermute x6, waiting for transfers between devices: 5.25 us -> 7.65 us  [rotate_img(): return lax.ppermute(value, 'img', perm)]
    dot_general x1, matrix products: 8.29 us -> 10.6 us  [on_device(): jnp.dot(onehot, table, precision=lax.Precision.HIGHEST, preferred_element...]
    ppermute x6, starting transfers between devices: 11.5 us -> 9.42 us  [rotate_img(): return lax.ppermute(value, 'img', perm)]
  transfers between devices with their start and end apart: 15 -> 19, of which waited for: 11 -> 8; matrix products, arithmetic and copies ran while one was open for 24% -> 28% of each run, Pallas kernels for 0% -> 6%
where the time goes in v2:
time: 111 us
  Pallas kernels  27.8 us (25%)
  waiting for transfers between devices  27.1 us (24%)
  starting transfers between devices  21.6 us (19%)
  local copies, waits for them, and re-layouts  19.8 us (18%)
  matrix products  10.6 us (10%)
  other arithmetic  2.67 us (2%)
  between operations  1.54 us (1%)
    slice x1, local copies, waits for them, and re-layouts, on_device(): images[0, :, part].astype(jnp.float32)  17.5 us
    pallas_call x2, Pallas kernels, project(): pl.pallas_call(functools.partial(projection_kernel, tile), out_shape=[chu...  14.4 us
    ppermute x6, waiting for transfers between devices, flip_cls(): lax.ppermute(value, 'cls', [(i, i ^ 1) for i in range(lax.axis_size('cls'...  13.9 us
    pallas_call x1, Pallas kernels, on_device(): pl.pallas_call(functools.partial(expectation_kernel, tile), out_shape=[ja...  13.4 us
    dot_general x1, matrix products, on_device(): jnp.dot(onehot, table, precision=lax.Precision.HIGHEST, preferred_element...  10.6 us
    ppermute x6, starting transfers between devices, rotate_img(): return lax.ppermute(value, 'img', perm)  9.42 us
    ppermute x6, waiting for transfers between devices, rotate_img(): return lax.ppermute(value, 'img', perm)  7.65 us
    ppermute x6, starting transfers between devices, flip_cls(): lax.ppermute(value, 'cls', [(i, i ^ 1) for i in range(lax.axis_size('cls'...  6.15 us
  transfers between devices with their start and end apart: 19, of which 8 were waited for; matrix products, arithmetic and copies ran while one was open for 28% of the time, Pallas kernels for 6%

profile of v2, /device:TPU:0, one launch (start us, length us, event | category | flops | bytes accessed | tf_op | source)
XLA Modules:
  0.0 111.1 jit_solution(8529910720769779518)
XLA Ops:
  0.6 0.9 copy.47
  1.6 3.1 %collective-permute-start = (bf16[2,32,1040]{2,1,0:T(8,128)(2,1)S(1)}, bf16[2,32,1040]{2,1,0:T(8,128)(2,1)S(1)}, u32[]{:S(2)}, u32[]{:S(2)}) collective-permute-start(bf16[2,32,1040]{2,1,0:T(8,128)(2,1)S(1)} %bitcast.89), channel_id=1, source_target_pairs={{0,2},{1,3},{2,4},{3,5},{4,6},{5,7},{6,0},{7,1},{8,10},{9,11},{10,... | collective-permute-start | bytes 399368 | tf_op jit(solution)/shard_map/ppermute | solution.py:45
  4.6 2.6 %collective-permute-start.1 = (bf16[2,32,1040]{2,1,0:T(8,128)(2,1)S(1)}, bf16[2,32,1040]{2,1,0:T(8,128)(2,1)S(1)}, u32[]{:S(2)}, u32[]{:S(2)}) collective-permute-start(bf16[2,32,1040]{2,1,0:T(8,128)(2,1)S(1)} %bitcast.90), channel_id=1, source_target_pairs={{0,4},{1,5},{2,6},{3,7},{4,0},{5,1},{6,2},{7,3},{8,12},{9,13},{10,... | collective-permute-start | bytes 399368 | tf_op jit(solution)/shard_map/ppermute | solution.py:45
  7.2 1.3 %collective-permute-start.2 = (bf16[2,32,1040]{2,1,0:T(8,128)(2,1)S(1)}, bf16[2,32,1040]{2,1,0:T(8,128)(2,1)S(1)}, u32[]{:S(2)}, u32[]{:S(2)}) collective-permute-start(bf16[2,32,1040]{2,1,0:T(8,128)(2,1)S(1)} %bitcast.91), channel_id=1, source_target_pairs={{0,6},{1,7},{2,0},{3,1},{4,2},{5,3},{6,4},{7,5},{8,14},{9,15},{10,... | collective-permute-start | bytes 399368 | tf_op jit(solution)/shard_map/ppermute | solution.py:45
  8.7 17.5 %fusion.32 = (bf16[1,256,1,8320]{3,2,1,0:T(2,128)(2,1)}, bf16[1,256,1,8320]{3,2,1,0:T(2,128)(2,1)}) fusion(bf16[1,256,2,8320]{3,2,1,0:T(2,128)(2,1)} %param.8), kind=kLoop, calls=%fused_computation.70 | loop fusion | bytes 17039360 | tf_op jit(solution)/shard_map/slice | solution.py:247
  26.2 1.0 fusion.6
  27.5 1.6 %collective-permute-start.3 = (bf16[4,32,1040]{2,1,0:T(8,128)(2,1)S(1)}, bf16[4,32,1040]{2,1,0:T(8,128)(2,1)S(1)}, u32[]{:S(2)}, u32[]{:S(2)}) collective-permute-start(bf16[4,32,1040]{2,1,0:T(8,128)(2,1)S(1)} %get-tuple-element.47.refs_0_), channel_id=1, source_target_pairs={{0,1},{1,0},{2,3},{3,2},{4,5},{5,4},{6,7},{7,6},{8,9},{9,8},{10,11... | collective-permute-start | bytes 798728 | tf_op jit(solution)/shard_map/ppermute | solution.py:35
  29.1 1.5 %collective-permute-start.4 = (bf16[4,32,1040]{2,1,0:T(8,128)(2,1)S(1)}, bf16[4,32,1040]{2,1,0:T(8,128)(2,1)S(1)}, u32[]{:S(2)}, u32[]{:S(2)}) collective-permute-start(bf16[4,32,1040]{2,1,0:T(8,128)(2,1)S(1)} %get-tuple-element.46.refs_4_), channel_id=1, source_target_pairs={{0,8},{8,0},{1,9},{9,1},{2,10},{10,2},{3,11},{11,3},{4,12},{12,4},... | collective-permute-start | bytes 798728 | tf_op jit(solution)/shard_map/ppermute | solution.py:39
  31.7 0.5 collective-permute-start.5
  32.2 0.5 collective-permute-start.7
  32.8 4.8 %collective-permute-done.3.refs_1_ = bf16[4,32,1040]{2,1,0:T(8,128)(2,1)S(1)} collective-permute-done((bf16[4,32,1040]{2,1,0:T(8,128)(2,1)S(1)}, bf16[4,32,1040]{2,1,0:T(8,128)(2,1)S(1)}, u32[]{:S(2)}, u32[]{:S(2)}) %collective-permute-start.3) | collective-permute-done | bytes 266272 | tf_op jit(solution)/shard_map/ppermute | solution.py:35
  37.5 1.5 %collective-permute-done.4.refs_6_ = bf16[4,32,1040]{2,1,0:T(8,128)(2,1)S(1)} collective-permute-done((bf16[4,32,1040]{2,1,0:T(8,128)(2,1)S(1)}, bf16[4,32,1040]{2,1,0:T(8,128)(2,1)S(1)}, u32[]{:S(2)}, u32[]{:S(2)}) %collective-permute-start.4) | collective-permute-done | bytes 266272 | tf_op jit(solution)/shard_map/ppermute | solution.py:39
  39.0 1.5 %collective-permute-start.6 = (bf16[4,32,1040]{2,1,0:T(8,128)(2,1)S(1)}, bf16[4,32,1040]{2,1,0:T(8,128)(2,1)S(1)}, u32[]{:S(2)}, u32[]{:S(2)}) collective-permute-start(bf16[4,32,1040]{2,1,0:T(8,128)(2,1)S(1)} %collective-permute-done.3.refs_1_), channel_id=1, source_target_pairs={{0,8},{8,0},{1,9},{9,1},{2,10},{10,2},{3,11},{11,3},{4,12},{12,4},... | collective-permute-start | bytes 798728 | tf_op jit(solution)/shard_map/ppermute | solution.py:39
  40.6 0.5 collective-permute-start.8
  41.1 10.6 %fusion = (bf16[256,8320]{1,0:T(8,128)(2,1)S(1)}, bf16[256,8320]{1,0:T(8,128)(2,1)S(1)}) fusion(bf16[1,256,1,8320]{3,2,1,0:T(2,128)(2,1)} %get-tuple-element.41, bf16[1,256,1,8320]{3,2,1,0:T(2,128)(2,1)} %get-tuple-element.42, f32[32,8320]{1,0:T(8,128)S(1)} %bitcast.85, s32[256]{0:T(256)S(1)} %bitcast.97), kind=kOutput, calls=%fused_computation.1 | convolution fusion | flops 830676992 | bytes 18105344 | tf_op jit(solution)/shard_map/dot_general | solution.py:243
  51.8 13.4 %shard_map.103 = (bf16[256,512]{1,0:T(8,128)(2,1)}, bf16[512,256]{1,0:T(8,128)(2,1)S(1)}) custom-call(s32[3]{0:T(128)S(1)} %pad_add_fusion.place_ref, s32[1]{0:T(128)} %bitcast.84.live_ref, s32[256,1]{1,0:T(8,128)S(1)} %copy.29.group_ref, s32[256,4]{1,0:T(8,128)S(1)} %bitcast.87, bf16[256,8320]{1,0:T(8,128)(2,1)S(1)} %get-tuple-element.40.wre_ref, ...), custom_call_target="tpu_custom_call" | custom-call | flops 4362076160 | bytes 8519680 | tf_op jit(solution)/shard_map/pallas_call | solution.py:255
  65.2 7.2 %shard_map.105 = (bf16[4,32,1040]{2,1,0:T(8,128)(2,1)S(1)}, bf16[4,32,1040]{2,1,0:T(8,128)(2,1)S(1)}, bf16[4,32,1040]{2,1,0:T(8,128)(2,1)S(1)}, bf16[4,32,1040]{2,1,0:T(8,128)(2,1)S(1)}) custom-call(s32[4]{0:T(128)S(1)} %pad_add_fusion.3.place_ref, bf16[512,256]{1,0:T(8,128)(2,1)S(1)} %get-tuple-element.20.turned_ref, ...), custom_call_target="tpu_custom_call" | custom-call | flops 136314880 | bytes 8519680 | tf_op jit(solution)/shard_map/pallas_call | solution.py:291
  72.4 1.6 %collective-permute-start.13 = (bf16[4,32,1040]{2,1,0:T(8,128)(2,1)S(1)}, bf16[4,32,1040]{2,1,0:T(8,128)(2,1)S(1)}, u32[]{:S(2)}, u32[]{:S(2)}) collective-permute-start(bf16[4,32,1040]{2,1,0:T(8,128)(2,1)S(1)} %get-tuple-element.28), channel_id=1, source_target_pairs={{0,1},{1,0},{2,3},{3,2},{4,5},{5,4},{6,7},{7,6},{8,9},{9,8},{10,11... | collective-permute-start | bytes 798728 | tf_op jit(solution)/shard_map/ppermute | solution.py:35
  73.9 7.2 %shard_map.104 = (bf16[4,32,1040]{2,1,0:T(8,128)(2,1)S(1)}, bf16[4,32,1040]{2,1,0:T(8,128)(2,1)S(1)}, bf16[4,32,1040]{2,1,0:T(8,128)(2,1)S(1)}, bf16[4,32,1040]{2,1,0:T(8,128)(2,1)S(1)}) custom-call(s32[4]{0:T(128)S(1)} %get-tuple-element.37.place_ref, bf16[512,256]{1,0:T(8,128)(2,1)S(1)} %get-tuple-element.20.turned_ref, ...), custom_call_target="tpu_custom_call" | custom-call | flops 136314880 | bytes 8519680 | tf_op jit(solution)/shard_map/pallas_call | solution.py:291
  81.2 0.6 collective-permute-start.12
  81.8 0.5 collective-permute-start.10
  82.3 1.5 %collective-permute-start.9 = (bf16[4,32,1040]{2,1,0:T(8,128)(2,1)S(1)}, bf16[4,32,1040]{2,1,0:T(8,128)(2,1)S(1)}, u32[]{:S(2)}, u32[]{:S(2)}) collective-permute-start(bf16[4,32,1040]{2,1,0:T(8,128)(2,1)S(1)} %get-tuple-element.22), channel_id=1, source_target_pairs={{0,8},{8,0},{1,9},{9,1},{2,10},{10,2},{3,11},{11,3},{4,12},{12,4},... | collective-permute-start | bytes 798728 | tf_op jit(solution)/shard_map/ppermute | solution.py:39
  83.9 0.6 collective-permute-start.14
  84.4 7.3 %collective-permute-done.10 = bf16[4,32,1040]{2,1,0:T(8,128)(2,1)S(1)} collective-permute-done((bf16[4,32,1040]{2,1,0:T(8,128)(2,1)S(1)}, bf16[4,32,1040]{2,1,0:T(8,128)(2,1)S(1)}, u32[]{:S(2)}, u32[]{:S(2)}) %collective-permute-start.10) | collective-permute-done | bytes 266272 | tf_op jit(solution)/shard_map/ppermute | solution.py:39
  91.8 1.2 %collective-permute-start.11 = (bf16[4,32,1040]{2,1,0:T(8,128)(2,1)S(1)}, bf16[4,32,1040]{2,1,0:T(8,128)(2,1)S(1)}, u32[]{:S(2)}, u32[]{:S(2)}) collective-permute-start(bf16[4,32,1040]{2,1,0:T(8,128)(2,1)S(1)} %add_convert_fusion.4), channel_id=1, source_target_pairs={{0,1},{1,0},{2,3},{3,2},{4,5},{5,4},{6,7},{7,6},{8,9},{9,8},{10,11... | collective-permute-start | bytes 798728 | tf_op jit(solution)/shard_map/ppermute | solution.py:35
  93.0 5.1 %collective-permute-done.14 = bf16[4,32,1040]{2,1,0:T(8,128)(2,1)S(1)} collective-permute-done((bf16[4,32,1040]{2,1,0:T(8,128)(2,1)S(1)}, bf16[4,32,1040]{2,1,0:T(8,128)(2,1)S(1)}, u32[]{:S(2)}, u32[]{:S(2)}) %collective-permute-start.14) | collective-permute-done | bytes 266272 | tf_op jit(solution)/shard_map/ppermute | solution.py:39
  98.8 0.5 collective-permute-start.15
  99.3 1.7 %collective-permute-start.16 = (bf16[2,32,1040]{2,1,0:T(8,128)(2,1)S(1)}, bf16[2,32,1040]{2,1,0:T(8,128)(2,1)S(1)}, u32[]{:S(2)}, u32[]{:S(2)}) collective-permute-start(bf16[2,32,1040]{2,1,0:T(8,128)(2,1)S(1)} %get-tuple-element.45), channel_id=1, source_target_pairs={{0,4},{1,5},{2,6},{3,7},{4,0},{5,1},{6,2},{7,3},{8,12},{9,13},{10,... | collective-permute-start | bytes 399368 | tf_op jit(solution)/shard_map/ppermute | solution.py:45
  101.2 2.8 %collective-permute-done.15 = bf16[2,32,1040]{2,1,0:T(8,128)(2,1)S(1)} collective-permute-done((bf16[2,32,1040]{2,1,0:T(8,128)(2,1)S(1)}, bf16[2,32,1040]{2,1,0:T(8,128)(2,1)S(1)}, u32[]{:S(2)}, u32[]{:S(2)}) %collective-permute-start.15) | collective-permute-done | bytes 133152 | tf_op jit(solution)/shard_map/ppermute | solution.py:45
  104.0 4.9 %collective-permute-done.16 = bf16[2,32,1040]{2,1,0:T(8,128)(2,1)S(1)} collective-permute-done((bf16[2,32,1040]{2,1,0:T(8,128)(2,1)S(1)}, bf16[2,32,1040]{2,1,0:T(8,128)(2,1)S(1)}, u32[]{:S(2)}, u32[]{:S(2)}) %collective-permute-start.16) | collective-permute-done | bytes 133152 | tf_op jit(solution)/shard_map/ppermute | solution.py:45
  109.0 0.9 copy.33
  110.4 0.7 fusion.15
  (41 shorter events, 2.4 us)
Async XLA Ops:
  1.6 25.8 %collective-permute-start = (bf16[2,32,1040]{2,1,0:T(8,128)(2,1)S(1)}, bf16[2,32,1040]{2,1,0:T(8,128)(2,1)S(1)}, u32[]{:S(2)}, u32[]{:S(2)}) collective-permute-start(bf16[2,32,1040]{2,1,0:T(8,128)(2,1)S(1)} %bitcast.89), channel_id=1, source_target_pairs={{0,2},{1,3},{2,4},{3,5},{4,6},{5,7},{6,0},{7,1},{8,10},{9,11},{10,... | collective-permute-start | bytes 399368 | tf_op jit(solution)/shard_map/ppermute | solution.py:45
  4.6 22.7 %collective-permute-start.1 = (bf16[2,32,1040]{2,1,0:T(8,128)(2,1)S(1)}, bf16[2,32,1040]{2,1,0:T(8,128)(2,1)S(1)}, u32[]{:S(2)}, u32[]{:S(2)}) collective-permute-start(bf16[2,32,1040]{2,1,0:T(8,128)(2,1)S(1)} %bitcast.90), channel_id=1, source_target_pairs={{0,4},{1,5},{2,6},{3,7},{4,0},{5,1},{6,2},{7,3},{8,12},{9,13},{10,... | collective-permute-start | bytes 399368 | tf_op jit(solution)/shard_map/ppermute | solution.py:45
  7.2 20.1 %collective-permute-start.2 = (bf16[2,32,1040]{2,1,0:T(8,128)(2,1)S(1)}, bf16[2,32,1040]{2,1,0:T(8,128)(2,1)S(1)}, u32[]{:S(2)}, u32[]{:S(2)}) collective-permute-start(bf16[2,32,1040]{2,1,0:T(8,128)(2,1)S(1)} %bitcast.91), channel_id=1, source_target_pairs={{0,6},{1,7},{2,0},{3,1},{4,2},{5,3},{6,4},{7,5},{8,14},{9,15},{10,... | collective-permute-start | bytes 399368 | tf_op jit(solution)/shard_map/ppermute | solution.py:45
  8.6 17.6 %copy-start.4 = (s32[1,8]{1,0:T(1,128)S(1)}, s32[1,8]{1,0:T(1,128)}, u32[]{:S(2)}) copy-start(s32[1,8]{1,0:T(1,128)} %param.13) | copy-start | bytes 100
  8.6 22.1 %copy-start.2 = (s32[1,256,4]{1,2,0:T(4,128)S(1)}, s32[1,256,4]{1,2,0:T(4,128)}, u32[]{:S(2)}) copy-start(s32[1,256,4]{1,2,0:T(4,128)} %param.12) | copy-start | bytes 12292
  8.6 22.2 %copy-start.3 = (s32[1,256]{1,0:T(1,128)S(1)}, s32[1,256]{1,0:T(1,128)}, u32[]{:S(2)}) copy-start(s32[1,256]{1,0:T(1,128)} %param.11) | copy-start | bytes 3076
  8.6 32.5 %copy-start = (f32[1,32,8320]{2,1,0:T(8,128)S(1)}, f32[1,32,8320]{2,1,0:T(8,128)}, u32[]{:S(2)}) copy-start(f32[1,32,8320]{2,1,0:T(8,128)} %param.10) | copy-start | bytes 3194884
  27.5 10.0 %collective-permute-start.3 = (bf16[4,32,1040]{2,1,0:T(8,128)(2,1)S(1)}, bf16[4,32,1040]{2,1,0:T(8,128)(2,1)S(1)}, u32[]{:S(2)}, u32[]{:S(2)}) collective-permute-start(bf16[4,32,1040]{2,1,0:T(8,128)(2,1)S(1)} %get-tuple-element.47.refs_0_), channel_id=1, source_target_pairs={{0,1},{1,0},{2,3},{3,2},{4,5},{5,4},{6,7},{7,6},{8,9},{9,8},{10,11... | collective-permute-start | bytes 798728 | tf_op jit(solution)/shard_map/ppermute | solution.py:35
  29.1 9.9 %collective-permute-start.4 = (bf16[4,32,1040]{2,1,0:T(8,128)(2,1)S(1)}, bf16[4,32,1040]{2,1,0:T(8,128)(2,1)S(1)}, u32[]{:S(2)}, u32[]{:S(2)}) collective-permute-start(bf16[4,32,1040]{2,1,0:T(8,128)(2,1)S(1)} %get-tuple-element.46.refs_4_), channel_id=1, source_target_pairs={{0,8},{8,0},{1,9},{9,1},{2,10},{10,2},{3,11},{11,3},{4,12},{12,4},... | collective-permute-start | bytes 798728 | tf_op jit(solution)/shard_map/ppermute | solution.py:39
  31.7 20.0 %collective-permute-start.5 = (bf16[4,32,1040]{2,1,0:T(8,128)(2,1)S(1)}, bf16[4,32,1040]{2,1,0:T(8,128)(2,1)S(1)}, u32[]{:S(2)}, u32[]{:S(2)}) collective-permute-start(bf16[4,32,1040]{2,1,0:T(8,128)(2,1)S(1)} %get-tuple-element.47.refs_0_), channel_id=1, source_target_pairs={{0,8},{8,0},{1,9},{9,1},{2,10},{10,2},{3,11},{11,3},{4,12},{12,4},... | collective-permute-start | bytes 798728 | tf_op jit(solution)/shard_map/ppermute | solution.py:39
  32.2 19.5 %collective-permute-start.7 = (bf16[4,32,1040]{2,1,0:T(8,128)(2,1)S(1)}, bf16[4,32,1040]{2,1,0:T(8,128)(2,1)S(1)}, u32[]{:S(2)}, u32[]{:S(2)}) collective-permute-start(bf16[4,32,1040]{2,1,0:T(8,128)(2,1)S(1)} %get-tuple-element.46.refs_4_), channel_id=1, source_target_pairs={{0,1},{1,0},{2,3},{3,2},{4,5},{5,4},{6,7},{7,6},{8,9},{9,8},{10,11... | collective-permute-start | bytes 798728 | tf_op jit(solution)/shard_map/ppermute | solution.py:35
  39.0 12.7 %collective-permute-start.6 = (bf16[4,32,1040]{2,1,0:T(8,128)(2,1)S(1)}, bf16[4,32,1040]{2,1,0:T(8,128)(2,1)S(1)}, u32[]{:S(2)}, u32[]{:S(2)}) collective-permute-start(bf16[4,32,1040]{2,1,0:T(8,128)(2,1)S(1)} %collective-permute-done.3.refs_1_), channel_id=1, source_target_pairs={{0,8},{8,0},{1,9},{9,1},{2,10},{10,2},{3,11},{11,3},{4,12},{12,4},... | collective-permute-start | bytes 798728 | tf_op jit(solution)/shard_map/ppermute | solution.py:39
  40.6 11.2 %collective-permute-start.8 = (bf16[4,32,1040]{2,1,0:T(8,128)(2,1)S(1)}, bf16[4,32,1040]{2,1,0:T(8,128)(2,1)S(1)}, u32[]{:S(2)}, u32[]{:S(2)}) collective-permute-start(bf16[4,32,1040]{2,1,0:T(8,128)(2,1)S(1)} %collective-permute-done.4.refs_6_), channel_id=1, source_target_pairs={{0,1},{1,0},{2,3},{3,2},{4,5},{5,4},{6,7},{7,6},{8,9},{9,8},{10,11... | collective-permute-start | bytes 798728 | tf_op jit(solution)/shard_map/ppermute | solution.py:35
  41.1 10.7 %copy-start.1 = (f32[1,8320]{1,0:T(1,128)S(1)}, f32[1,8320]{1,0:T(1,128)}, u32[]{:S(2)}) copy-start(f32[1,8320]{1,0:T(1,128)} %refs_9_.1) | copy-start | bytes 99844
  72.4 11.4 %collective-permute-start.13 = (bf16[4,32,1040]{2,1,0:T(8,128)(2,1)S(1)}, bf16[4,32,1040]{2,1,0:T(8,128)(2,1)S(1)}, u32[]{:S(2)}, u32[]{:S(2)}) collective-permute-start(bf16[4,32,1040]{2,1,0:T(8,128)(2,1)S(1)} %get-tuple-element.28), channel_id=1, source_target_pairs={{0,1},{1,0},{2,3},{3,2},{4,5},{5,4},{6,7},{7,6},{8,9},{9,8},{10,11... | collective-permute-start | bytes 798728 | tf_op jit(solution)/shard_map/ppermute | solution.py:35
  81.2 11.8 %collective-permute-start.12 = (bf16[4,32,1040]{2,1,0:T(8,128)(2,1)S(1)}, bf16[4,32,1040]{2,1,0:T(8,128)(2,1)S(1)}, u32[]{:S(2)}, u32[]{:S(2)}) collective-permute-start(bf16[4,32,1040]{2,1,0:T(8,128)(2,1)S(1)} %get-tuple-element.26), channel_id=1, source_target_pairs={{0,1},{1,0},{2,3},{3,2},{4,5},{5,4},{6,7},{7,6},{8,9},{9,8},{10,11... | collective-permute-start | bytes 798728 | tf_op jit(solution)/shard_map/ppermute | solution.py:35
  81.8 9.9 %collective-permute-start.10 = (bf16[4,32,1040]{2,1,0:T(8,128)(2,1)S(1)}, bf16[4,32,1040]{2,1,0:T(8,128)(2,1)S(1)}, u32[]{:S(2)}, u32[]{:S(2)}) collective-permute-start(bf16[4,32,1040]{2,1,0:T(8,128)(2,1)S(1)} %get-tuple-element.24), channel_id=1, source_target_pairs={{0,8},{8,0},{1,9},{9,1},{2,10},{10,2},{3,11},{11,3},{4,12},{12,4},... | collective-permute-start | bytes 798728 | tf_op jit(solution)/shard_map/ppermute | solution.py:39
  82.3 16.0 %collective-permute-start.9 = (bf16[4,32,1040]{2,1,0:T(8,128)(2,1)S(1)}, bf16[4,32,1040]{2,1,0:T(8,128)(2,1)S(1)}, u32[]{:S(2)}, u32[]{:S(2)}) collective-permute-start(bf16[4,32,1040]{2,1,0:T(8,128)(2,1)S(1)} %get-tuple-element.22), channel_id=1, source_target_pairs={{0,8},{8,0},{1,9},{9,1},{2,10},{10,2},{3,11},{11,3},{4,12},{12,4},... | collective-permute-start | bytes 798728 | tf_op jit(solution)/shard_map/ppermute | solution.py:39
  83.9 14.2 %collective-permute-start.14 = (bf16[4,32,1040]{2,1,0:T(8,128)(2,1)S(1)}, bf16[4,32,1040]{2,1,0:T(8,128)(2,1)S(1)}, u32[]{:S(2)}, u32[]{:S(2)}) collective-permute-start(bf16[4,32,1040]{2,1,0:T(8,128)(2,1)S(1)} %add_convert_fusion.1), channel_id=1, source_target_pairs={{0,8},{8,0},{1,9},{9,1},{2,10},{10,2},{3,11},{11,3},{4,12},{12,4},... | collective-permute-start | bytes 798728 | tf_op jit(solution)/shard_map/ppermute | solution.py:39
  91.8 6.8 %collective-permute-start.11 = (bf16[4,32,1040]{2,1,0:T(8,128)(2,1)S(1)}, bf16[4,32,1040]{2,1,0:T(8,128)(2,1)S(1)}, u32[]{:S(2)}, u32[]{:S(2)}) collective-permute-start(bf16[4,32,1040]{2,1,0:T(8,128)(2,1)S(1)} %add_convert_fusion.4), channel_id=1, source_target_pairs={{0,1},{1,0},{2,3},{3,2},{4,5},{5,4},{6,7},{7,6},{8,9},{9,8},{10,11... | collective-permute-start | bytes 798728 | tf_op jit(solution)/shard_map/ppermute | solution.py:35
  98.8 5.2 %collective-permute-start.15 = (bf16[2,32,1040]{2,1,0:T(8,128)(2,1)S(1)}, bf16[2,32,1040]{2,1,0:T(8,128)(2,1)S(1)}, u32[]{:S(2)}, u32[]{:S(2)}) collective-permute-start(bf16[2,32,1040]{2,1,0:T(8,128)(2,1)S(1)} %get-tuple-element.43), channel_id=1, source_target_pairs={{0,6},{1,7},{2,0},{3,1},{4,2},{5,3},{6,4},{7,5},{8,14},{9,15},{10,... | collective-permute-start | bytes 399368 | tf_op jit(solution)/shard_map/ppermute | solution.py:45
  99.3 9.5 %collective-permute-start.16 = (bf16[2,32,1040]{2,1,0:T(8,128)(2,1)S(1)}, bf16[2,32,1040]{2,1,0:T(8,128)(2,1)S(1)}, u32[]{:S(2)}, u32[]{:S(2)}) collective-permute-start(bf16[2,32,1040]{2,1,0:T(8,128)(2,1)S(1)} %get-tuple-element.45), channel_id=1, source_target_pairs={{0,4},{1,5},{2,6},{3,7},{4,0},{5,1},{6,2},{7,3},{8,12},{9,13},{10,... | collective-permute-start | bytes 399368 | tf_op jit(solution)/shard_map/ppermute | solution.py:45
  101.0 7.9 %collective-permute-start.17 = (bf16[2,32,1040]{2,1,0:T(8,128)(2,1)S(1)}, bf16[2,32,1040]{2,1,0:T(8,128)(2,1)S(1)}, u32[]{:S(2)}, u32[]{:S(2)}) collective-permute-start(bf16[2,32,1040]{2,1,0:T(8,128)(2,1)S(1)} %get-tuple-element.44), channel_id=1, source_target_pairs={{0,2},{1,3},{2,4},{3,5},{4,6},{5,7},{6,0},{7,1},{8,10},{9,11},{10,... | collective-permute-start | bytes 399368 | tf_op jit(solution)/shard_map/ppermute | solution.py:45
  108.9 1.4 %collective-permute-start.18 = (bf16[2,32,1040]{2,1,0:T(8,128)(2,1)S(1)}, bf16[2,32,1040]{2,1,0:T(8,128)(2,1)S(1)}, u32[]{:S(2)}, u32[]{:S(2)}) collective-permute-start(bf16[2,32,1040]{2,1,0:T(8,128)(2,1)S(1)} %get-tuple-element.35), channel_id=1, source_target_pairs={{0,16},{16,0},{1,17},{17,1},{2,18},{18,2},{3,19},{19,3},{4,20},{20... | collective-permute-start | bytes 399368 | tf_op jit(solution)/shard_map/ppermute | solution.py:321

commit v3 on v2

--- a/solution.py
+++ b/solution.py
@@ -158,16 +158,14 @@
     wim_ref,
     cos_ref,
     sin_ref,
-    out_re_same,
-    out_re_other,
-    out_im_same,
-    out_im_other,
+    out_same,
+    out_other,
     slab_re,
     slab_im,
 ):
     freqs = wre_ref.shape[1]
     trans = cos_ref.shape[0]
-    lines, owned, width = out_re_same.shape
+    lines, _, owned, width = out_same.shape
     sections = turned_ref.shape[0] // trans
     my_line, my_side, chosen = place_ref[1], place_ref[2], place_ref[3]
     weights = jnp.concatenate(
@@ -204,13 +202,13 @@
 
         @pl.when(side == 0)
         def _():
-            out_re_same[step] = chunk_re
-            out_im_same[step] = chunk_im
+            out_same[step, 0] = chunk_re
+            out_same[step, 1] = chunk_im
 
         @pl.when(side != 0)
         def _():
-            out_re_other[step] = chunk_re
-            out_im_other[step] = chunk_im
+            out_other[step, 0] = chunk_re
+            out_other[step, 1] = chunk_im
 
 
 def on_device(images, projections, ctf_table, ctf_group, orient_ids, trans_ids, inv_sigma, counts):
@@ -229,6 +227,7 @@
 
     own = projections[0].reshape(owned, 2, width).transpose(1, 0, 2)
     line = jnp.stack([own] + [rotate_img(own, s) for s in range(1, lines)], axis=1)
+    early_table, line = lax.optimization_barrier((ctf_table[0], line))
     same_re, same_im = line[0], line[1]
     side_re = flip_img(same_re)
     far_im = flip_cls(same_im)
@@ -240,13 +239,14 @@
     onehot = (ctf_group[0][:, None] == jnp.arange(groups, dtype=jnp.int32)[None, :]).astype(
         jnp.float32
     )
-    ctf_rows = jnp.dot(
-        onehot, table, precision=lax.Precision.HIGHEST, preferred_element_type=jnp.float32
-    )
-    weighted = [
-        (ctf_rows * images[0, :, part].astype(jnp.float32)).astype(jnp.bfloat16)
-        for part in range(2)
-    ]
+    weighted = []
+    for part, values in enumerate((table, early_table)):
+        ctf_rows = jnp.dot(
+            onehot, values, precision=lax.Precision.HIGHEST, preferred_element_type=jnp.float32
+        )
+        weighted.append(
+            (ctf_rows * images[0, :, part].astype(jnp.float32)).astype(jnp.bfloat16)
+        )
     cosine, sine = phases(trans_ids[0], freqs)
 
     place_mine = [cls_index, img_index // 2, img_index % 2]
@@ -287,12 +287,12 @@
     )
 
     def project(chosen):
-        chunks = jax.ShapeDtypeStruct((lines, owned, width), jnp.bfloat16)
+        chunks = jax.ShapeDtypeStruct((lines, 2, owned, width), jnp.bfloat16)
         return pl.pallas_call(
             functools.partial(projection_kernel, tile),
-            out_shape=[chunks] * 4,
+            out_shape=[chunks] * 2,
             in_specs=[smem] + [vmem] * 5,
-            out_specs=[vmem] * 4,
+            out_specs=[vmem] * 2,
             scratch_shapes=[
                 pltpu.VMEM((owned, freqs), jnp.bfloat16),
                 pltpu.VMEM((owned, freqs), jnp.bfloat16),
@@ -305,16 +305,11 @@
             ),
         )(jnp.stack(place_mine + [chosen]).astype(jnp.int32), turned, *weighted, cosine, sine)
 
-    far_re_same, far_re_other, far_im_same, far_im_other = project(1 - cls_index)
-    near_re_same, near_re_other, near_im_same, near_im_other = project(cls_index)
-
-    other_re = add_rounded(near_re_other, flip_cls(far_re_other))
-    sum_im_far = add_rounded(far_im_same, flip_img(far_im_other))
-    same_sum = add_rounded(near_re_same, flip_cls(far_re_same))
-    sum_im_near = add_rounded(near_im_same, flip_img(near_im_other))
-    line_re = add_rounded(same_sum, flip_img(other_re))
-    line_im = add_rounded(sum_im_near, flip_cls(sum_im_far))
-    lines_both = jnp.stack([line_re, line_im], axis=1)
+    far_same, far_other = project(1 - cls_index)
+    near_same, near_other = project(cls_index)
+    sum_far = add_rounded(far_same, flip_img(far_other))
+    sum_near = add_rounded(near_same, flip_img(near_other))
+    lines_both = add_rounded(sum_near, flip_cls(sum_far))
     own_slab = lines_both[0].astype(jnp.float32)
     for s in range(1, lines):
         own_slab = own_slab + rotate_img(lines_both[s], lines - s).astype(jnp.float32)

time: 111 us -> 112 us (level)
  starting transfers between devices: 21.6 us -> 18.5 us
  waiting for transfers between devices: 27.1 us -> 29.7 us
  matrix products: 10.6 us -> 12.1 us
    ppermute x6 -> x5, waiting for transfers between devices: 5.14 us -> 15.9 us  [flip_img(): lax.ppermute(value, 'img', [(i, i ^ 1) for i in range(lax.axis_size('img'...]
    ppermute x6 -> x4, waiting for transfers between devices: 13.9 us -> 5.82 us  [flip_cls(): lax.ppermute(value, 'cls', [(i, i ^ 1) for i in range(lax.axis_size('cls'...]
    ppermute x6 -> x4, starting transfers between devices: 6.15 us -> 4.12 us  [flip_cls(): lax.ppermute(value, 'cls', [(i, i ^ 1) for i in range(lax.axis_size('cls'...]
    dot_general x1 -> x2, matrix products: 10.6 us -> 12.1 us  [on_device(): jnp.dot(onehot, values, precision=lax.Precision.HIGHEST, preferred_elemen...]
    ppermute x6 -> x5, starting transfers between devices: 5.97 us -> 4.78 us  [flip_img(): lax.ppermute(value, 'img', [(i, i ^ 1) for i in range(lax.axis_size('img'...]
  transfers between devices with their start and end apart: 19 -> 16, of which waited for: 8 -> 8; matrix products, arithmetic and copies ran while one was open for 28% -> 29% of each run, Pallas kernels for 6% -> 6%
where the time goes in v3:
time: 112 us
  waiting for transfers between devices  29.7 us (27%)
  Pallas kernels  27.8 us (25%)
  local copies, waits for them, and re-layouts  19.8 us (18%)
  starting transfers between devices  18.5 us (17%)
  matrix products  12.1 us (11%)
  other arithmetic  2.55 us (2%)
  between operations  1.54 us (1%)
    slice x1, local copies, waits for them, and re-layouts, on_device(): images[0, :, part].astype(jnp.float32)  17.5 us
    ppermute x5, waiting for transfers between devices, flip_img(): lax.ppermute(value, 'img', [(i, i ^ 1) for i in range(lax.axis_size('img'...  15.9 us
    pallas_call x2, Pallas kernels, project(): pl.pallas_call(functools.partial(projection_kernel, tile), out_shape=[chu...  14.6 us
    pallas_call x1, Pallas kernels, on_device(): pl.pallas_call(functools.partial(expectation_kernel, tile), out_shape=[ja...  13.2 us
    dot_general x2, matrix products, on_device(): jnp.dot(onehot, values, precision=lax.Precision.HIGHEST, preferred_elemen...  12.1 us
    ppermute x6, starting transfers between devices, rotate_img(): return lax.ppermute(value, 'img', perm)  9.56 us
    ppermute x6, waiting for transfers between devices, rotate_img(): return lax.ppermute(value, 'img', perm)  7.5 us
    ppermute x4, waiting for transfers between devices, flip_cls(): lax.ppermute(value, 'cls', [(i, i ^ 1) for i in range(lax.axis_size('cls'...  5.82 us
  transfers between devices with their start and end apart: 16, of which 8 were waited for; matrix products, arithmetic and copies ran while one was open for 29% of the time, Pallas kernels for 6%

profile of v3, /device:TPU:0, one launch (start us, length us, event | category | flops | bytes accessed | tf_op | source)
XLA Modules:
  0.0 112.0 jit_solution(3150844919754561160)
XLA Ops:
  0.6 0.9 copy.38
  1.6 3.1 %collective-permute-start = (bf16[2,32,1040]{2,1,0:T(8,128)(2,1)S(1)}, bf16[2,32,1040]{2,1,0:T(8,128)(2,1)S(1)}, u32[]{:S(2)}, u32[]{:S(2)}) collective-permute-start(bf16[2,32,1040]{2,1,0:T(8,128)(2,1)S(1)} %bitcast.81), channel_id=1, source_target_pairs={{0,2},{1,3},{2,4},{3,5},{4,6},{5,7},{6,0},{7,1},{8,10},{9,11},{10,... | collective-permute-start | bytes 399368 | tf_op jit(solution)/shard_map/ppermute | solution.py:45
  4.6 2.6 %collective-permute-start.1 = (bf16[2,32,1040]{2,1,0:T(8,128)(2,1)S(1)}, bf16[2,32,1040]{2,1,0:T(8,128)(2,1)S(1)}, u32[]{:S(2)}, u32[]{:S(2)}) collective-permute-start(bf16[2,32,1040]{2,1,0:T(8,128)(2,1)S(1)} %bitcast.82), channel_id=1, source_target_pairs={{0,4},{1,5},{2,6},{3,7},{4,0},{5,1},{6,2},{7,3},{8,12},{9,13},{10,... | collective-permute-start | bytes 399368 | tf_op jit(solution)/shard_map/ppermute | solution.py:45
  7.2 1.3 %collective-permute-start.2 = (bf16[2,32,1040]{2,1,0:T(8,128)(2,1)S(1)}, bf16[2,32,1040]{2,1,0:T(8,128)(2,1)S(1)}, u32[]{:S(2)}, u32[]{:S(2)}) collective-permute-start(bf16[2,32,1040]{2,1,0:T(8,128)(2,1)S(1)} %bitcast.83), channel_id=1, source_target_pairs={{0,6},{1,7},{2,0},{3,1},{4,2},{5,3},{6,4},{7,5},{8,14},{9,15},{10,... | collective-permute-start | bytes 399368 | tf_op jit(solution)/shard_map/ppermute | solution.py:45
  8.7 17.5 %fusion.23 = (bf16[1,256,1,8320]{3,2,1,0:T(2,128)(2,1)}, bf16[1,256,1,8320]{3,2,1,0:T(2,128)(2,1)}) fusion(bf16[1,256,2,8320]{3,2,1,0:T(2,128)(2,1)} %param.8), kind=kLoop, calls=%fused_computation.55 | loop fusion | bytes 17039360 | tf_op jit(solution)/shard_map/slice | solution.py:248
  26.3 1.0 fusion.4
  28.7 1.6 %collective-permute-start.3 = (bf16[4,32,1040]{2,1,0:T(8,128)(2,1)S(1)}, bf16[4,32,1040]{2,1,0:T(8,128)(2,1)S(1)}, u32[]{:S(2)}, u32[]{:S(2)}) collective-permute-start(bf16[4,32,1040]{2,1,0:T(8,128)(2,1)S(1)} %get-tuple-element.41.refs_0_), channel_id=1, source_target_pairs={{0,1},{1,0},{2,3},{3,2},{4,5},{5,4},{6,7},{7,6},{8,9},{9,8},{10,11... | collective-permute-start | bytes 798728 | tf_op jit(solution)/shard_map/ppermute | solution.py:35
  30.2 1.5 %collective-permute-start.5 = (bf16[4,32,1040]{2,1,0:T(8,128)(2,1)S(1)}, bf16[4,32,1040]{2,1,0:T(8,128)(2,1)S(1)}, u32[]{:S(2)}, u32[]{:S(2)}) collective-permute-start(bf16[4,32,1040]{2,1,0:T(8,128)(2,1)S(1)} %get-tuple-element.41.refs_0_), channel_id=1, source_target_pairs={{0,8},{8,0},{1,9},{9,1},{2,10},{10,2},{3,11},{11,3},{4,12},{12,4},... | collective-permute-start | bytes 798728 | tf_op jit(solution)/shard_map/ppermute | solution.py:39
  31.7 0.5 collective-permute-start.4
  32.2 0.5 collective-permute-start.7
  32.8 7.4 %fusion.1.wim_ref = bf16[256,8320]{1,0:T(8,128)(2,1)S(1)} fusion(f32[32,8320]{1,0:T(8,128)S(1)} %bitcast.76, bf16[1,256,1,8320]{3,2,1,0:T(2,128)(2,1)} %get-tuple-element.35, s32[256]{0:T(256)S(1)} %bitcast.89), kind=kOutput, calls=%fused_computation.3 | convolution fusion | flops 824287232 | bytes 9585664 | tf_op jit(solution)/shard_map/dot_general | solution.py:244
  40.2 4.0 %collective-permute-done.4.refs_6_ = bf16[4,32,1040]{2,1,0:T(8,128)(2,1)S(1)} collective-permute-done((bf16[4,32,1040]{2,1,0:T(8,128)(2,1)S(1)}, bf16[4,32,1040]{2,1,0:T(8,128)(2,1)S(1)}, u32[]{:S(2)}, u32[]{:S(2)}) %collective-permute-start.4) | collective-permute-done | bytes 266272 | tf_op jit(solution)/shard_map/ppermute | solution.py:39
  44.2 1.5 %collective-permute-start.6 = (bf16[4,32,1040]{2,1,0:T(8,128)(2,1)S(1)}, bf16[4,32,1040]{2,1,0:T(8,128)(2,1)S(1)}, u32[]{:S(2)}, u32[]{:S(2)}) collective-permute-start(bf16[4,32,1040]{2,1,0:T(8,128)(2,1)S(1)} %collective-permute-done.3.refs_1_), channel_id=1, source_target_pairs={{0,8},{8,0},{1,9},{9,1},{2,10},{10,2},{3,11},{11,3},{4,12},{12,4},... | collective-permute-start | bytes 798728 | tf_op jit(solution)/shard_map/ppermute | solution.py:39
  45.7 0.5 collective-permute-start.8
  46.2 4.7 %fusion.wre_ref = bf16[256,8320]{1,0:T(8,128)(2,1)S(1)} fusion(f32[32,8320]{1,0:T(8,128)S(1)} %bitcast.77, bf16[1,256,1,8320]{3,2,1,0:T(2,128)(2,1)S(1)} %copy-done.2, s32[256]{0:T(256)S(1)} %bitcast.90), kind=kOutput, calls=%fused_computation.2 | convolution fusion | flops 824287232 | bytes 9585664 | tf_op jit(solution)/shard_map/dot_general | solution.py:244
  51.0 1.4 %collective-permute-done.8.refs_7_ = bf16[4,32,1040]{2,1,0:T(8,128)(2,1)S(1)} collective-permute-done((bf16[4,32,1040]{2,1,0:T(8,128)(2,1)S(1)}, bf16[4,32,1040]{2,1,0:T(8,128)(2,1)S(1)}, u32[]{:S(2)}, u32[]{:S(2)}) %collective-permute-start.8) | collective-permute-done | bytes 266272 | tf_op jit(solution)/shard_map/ppermute | solution.py:35
  52.4 13.2 %shard_map.103 = (bf16[256,512]{1,0:T(8,128)(2,1)}, bf16[512,256]{1,0:T(8,128)(2,1)S(1)}) custom-call(s32[3]{0:T(128)S(1)} %pad_add_fusion.place_ref, s32[1]{0:T(128)} %bitcast.75.live_ref, s32[256,1]{1,0:T(8,128)S(1)} %copy.26.group_ref, s32[256,4]{1,0:T(8,128)S(1)} %bitcast.79, bf16[256,8320]{1,0:T(8,128)(2,1)S(1)} %fusion.wre_ref, ...), custom_call_target="tpu_custom_call" | custom-call | flops 4362076160 | bytes 8519680 | tf_op jit(solution)/shard_map/pallas_call | solution.py:255
  65.6 7.4 %shard_map.105 = (bf16[4,2,32,1040]{3,2,1,0:T(8,128)(2,1)S(1)}, bf16[4,2,32,1040]{3,2,1,0:T(8,128)(2,1)S(1)}) custom-call(s32[4]{0:T(128)S(1)} %pad_add_fusion.3.place_ref, bf16[512,256]{1,0:T(8,128)(2,1)S(1)} %get-tuple-element.20.turned_ref, bf16[256,8320]{1,0:T(8,128)(2,1)S(1)} %fusion.wre_ref, bf16[256,8320]{1,0:T(8,128)(2,1)S(1)} %fusion.1.wim_ref, ...), custom_call_target="tpu_custom_call" | custom-call | flops 136314880 | bytes 8519680 | tf_op jit(solution)/shard_map/pallas_call | solution.py:291
  73.0 0.6 collective-permute-start.10
  73.6 7.2 %shard_map.104 = (bf16[4,2,32,1040]{3,2,1,0:T(8,128)(2,1)S(1)}, bf16[4,2,32,1040]{3,2,1,0:T(8,128)(2,1)S(1)}) custom-call(s32[4]{0:T(128)S(1)} %get-tuple-element.33.place_ref, bf16[512,256]{1,0:T(8,128)(2,1)S(1)} %get-tuple-element.20.turned_ref, bf16[256,8320]{1,0:T(8,128)(2,1)S(1)} %fusion.wre_ref, bf16[256,8320]{1,0:T(8,128)(2,1)S(1)} %fusion.1.wim_ref, ...), custom_call_target="tpu_custom_call" | custom-call | flops 136314880 | bytes 8519680 | tf_op jit(solution)/shard_map/pallas_call | solution.py:291
  80.8 1.6 %collective-permute-start.9 = (bf16[4,2,32,1040]{3,2,1,0:T(8,128)(2,1)S(1)}, bf16[4,2,32,1040]{3,2,1,0:T(8,128)(2,1)S(1)}, u32[]{:S(2)}, u32[]{:S(2)}) collective-permute-start(bf16[4,2,32,1040]{3,2,1,0:T(8,128)(2,1)S(1)} %get-tuple-element.22), channel_id=1, source_target_pairs={{0,1},{1,0},{2,3},{3,2},{4,5},{5,4},{6,7},{7,6},{8,9},{9,8},{10,11... | collective-permute-start | bytes 1597448 | tf_op jit(solution)/shard_map/ppermute | solution.py:35
  82.4 7.0 %collective-permute-done.10 = bf16[4,2,32,1040]{3,2,1,0:T(8,128)(2,1)S(1)} collective-permute-done((bf16[4,2,32,1040]{3,2,1,0:T(8,128)(2,1)S(1)}, bf16[4,2,32,1040]{3,2,1,0:T(8,128)(2,1)S(1)}, u32[]{:S(2)}, u32[]{:S(2)}) %collective-permute-start.10) | collective-permute-done | bytes 532512 | tf_op jit(solution)/shard_map/ppermute | solution.py:35
  89.5 0.6 collective-permute-start.11
  90.1 7.5 %collective-permute-done.9 = bf16[4,2,32,1040]{3,2,1,0:T(8,128)(2,1)S(1)} collective-permute-done((bf16[4,2,32,1040]{3,2,1,0:T(8,128)(2,1)S(1)}, bf16[4,2,32,1040]{3,2,1,0:T(8,128)(2,1)S(1)}, u32[]{:S(2)}, u32[]{:S(2)}) %collective-permute-start.9) | collective-permute-done | bytes 532512 | tf_op jit(solution)/shard_map/ppermute | solution.py:35
  97.6 1.8 %collective-permute-done.11 = bf16[4,2,32,1040]{3,2,1,0:T(8,128)(2,1)S(1)} collective-permute-done((bf16[4,2,32,1040]{3,2,1,0:T(8,128)(2,1)S(1)}, bf16[4,2,32,1040]{3,2,1,0:T(8,128)(2,1)S(1)}, u32[]{:S(2)}, u32[]{:S(2)}) %collective-permute-start.11) | collective-permute-done | bytes 532512 | tf_op jit(solution)/shard_map/ppermute | solution.py:39
  99.7 0.5 collective-permute-start.12
  100.2 1.7 %collective-permute-start.13 = (bf16[2,32,1040]{2,1,0:T(8,128)(2,1)S(1)}, bf16[2,32,1040]{2,1,0:T(8,128)(2,1)S(1)}, u32[]{:S(2)}, u32[]{:S(2)}) collective-permute-start(bf16[2,32,1040]{2,1,0:T(8,128)(2,1)S(1)} %get-tuple-element.39), channel_id=1, source_target_pairs={{0,4},{1,5},{2,6},{3,7},{4,0},{5,1},{6,2},{7,3},{8,12},{9,13},{10,... | collective-permute-start | bytes 399368 | tf_op jit(solution)/shard_map/ppermute | solution.py:45
  102.3 2.6 %collective-permute-done.12 = bf16[2,32,1040]{2,1,0:T(8,128)(2,1)S(1)} collective-permute-done((bf16[2,32,1040]{2,1,0:T(8,128)(2,1)S(1)}, bf16[2,32,1040]{2,1,0:T(8,128)(2,1)S(1)}, u32[]{:S(2)}, u32[]{:S(2)}) %collective-permute-start.12) | collective-permute-done | bytes 133152 | tf_op jit(solution)/shard_map/ppermute | solution.py:45
  104.9 4.8 %collective-permute-done.13 = bf16[2,32,1040]{2,1,0:T(8,128)(2,1)S(1)} collective-permute-done((bf16[2,32,1040]{2,1,0:T(8,128)(2,1)S(1)}, bf16[2,32,1040]{2,1,0:T(8,128)(2,1)S(1)}, u32[]{:S(2)}, u32[]{:S(2)}) %collective-permute-start.13) | collective-permute-done | bytes 133152 | tf_op jit(solution)/shard_map/ppermute | solution.py:45
  109.9 0.9 copy.27
  110.9 0.4 collective-permute-done.15
  111.3 0.7 fusion.7
  (36 shorter events, 1.7 us)
Async XLA Ops:
  1.6 26.9 %collective-permute-start = (bf16[2,32,1040]{2,1,0:T(8,128)(2,1)S(1)}, bf16[2,32,1040]{2,1,0:T(8,128)(2,1)S(1)}, u32[]{:S(2)}, u32[]{:S(2)}) collective-permute-start(bf16[2,32,1040]{2,1,0:T(8,128)(2,1)S(1)} %bitcast.81), channel_id=1, source_target_pairs={{0,2},{1,3},{2,4},{3,5},{4,6},{5,7},{6,0},{7,1},{8,10},{9,11},{10,... | collective-permute-start | bytes 399368 | tf_op jit(solution)/shard_map/ppermute | solution.py:45
  4.6 23.8 %collective-permute-start.1 = (bf16[2,32,1040]{2,1,0:T(8,128)(2,1)S(1)}, bf16[2,32,1040]{2,1,0:T(8,128)(2,1)S(1)}, u32[]{:S(2)}, u32[]{:S(2)}) collective-permute-start(bf16[2,32,1040]{2,1,0:T(8,128)(2,1)S(1)} %bitcast.82), channel_id=1, source_target_pairs={{0,4},{1,5},{2,6},{3,7},{4,0},{5,1},{6,2},{7,3},{8,12},{9,13},{10,... | collective-permute-start | bytes 399368 | tf_op jit(solution)/shard_map/ppermute | solution.py:45
  7.2 21.3 %collective-permute-start.2 = (bf16[2,32,1040]{2,1,0:T(8,128)(2,1)S(1)}, bf16[2,32,1040]{2,1,0:T(8,128)(2,1)S(1)}, u32[]{:S(2)}, u32[]{:S(2)}) collective-permute-start(bf16[2,32,1040]{2,1,0:T(8,128)(2,1)S(1)} %bitcast.83), channel_id=1, source_target_pairs={{0,6},{1,7},{2,0},{3,1},{4,2},{5,3},{6,4},{7,5},{8,14},{9,15},{10,... | collective-permute-start | bytes 399368 | tf_op jit(solution)/shard_map/ppermute | solution.py:45
  8.6 17.6 %copy-start.5 = (s32[1,8]{1,0:T(1,128)S(1)}, s32[1,8]{1,0:T(1,128)}, u32[]{:S(2)}) copy-start(s32[1,8]{1,0:T(1,128)} %param.13) | copy-start | bytes 100
  8.6 18.8 %copy-start.4 = (s32[1,256,4]{1,2,0:T(4,128)S(1)}, s32[1,256,4]{1,2,0:T(4,128)}, u32[]{:S(2)}) copy-start(s32[1,256,4]{1,2,0:T(4,128)} %param.12) | copy-start | bytes 12292
  8.6 18.9 %copy-start.3 = (s32[1,256]{1,0:T(1,128)S(1)}, s32[1,256]{1,0:T(1,128)}, u32[]{:S(2)}) copy-start(s32[1,256]{1,0:T(1,128)} %param.11) | copy-start | bytes 3076
  8.7 24.1 %copy-start = (f32[1,32,8320]{2,1,0:T(8,128)S(1)}, f32[1,32,8320]{2,1,0:T(8,128)}, u32[]{:S(2)}) copy-start(f32[1,32,8320]{2,1,0:T(8,128)} %param.10) | copy-start | bytes 3194884
  28.7 11.5 %collective-permute-start.3 = (bf16[4,32,1040]{2,1,0:T(8,128)(2,1)S(1)}, bf16[4,32,1040]{2,1,0:T(8,128)(2,1)S(1)}, u32[]{:S(2)}, u32[]{:S(2)}) collective-permute-start(bf16[4,32,1040]{2,1,0:T(8,128)(2,1)S(1)} %get-tuple-element.41.refs_0_), channel_id=1, source_target_pairs={{0,1},{1,0},{2,3},{3,2},{4,5},{5,4},{6,7},{7,6},{8,9},{9,8},{10,11... | collective-permute-start | bytes 798728 | tf_op jit(solution)/shard_map/ppermute | solution.py:35
  30.2 20.7 %collective-permute-start.5 = (bf16[4,32,1040]{2,1,0:T(8,128)(2,1)S(1)}, bf16[4,32,1040]{2,1,0:T(8,128)(2,1)S(1)}, u32[]{:S(2)}, u32[]{:S(2)}) collective-permute-start(bf16[4,32,1040]{2,1,0:T(8,128)(2,1)S(1)} %get-tuple-element.41.refs_0_), channel_id=1, source_target_pairs={{0,8},{8,0},{1,9},{9,1},{2,10},{10,2},{3,11},{11,3},{4,12},{12,4},... | collective-permute-start | bytes 798728 | tf_op jit(solution)/shard_map/ppermute | solution.py:39
  31.7 12.4 %collective-permute-start.4 = (bf16[4,32,1040]{2,1,0:T(8,128)(2,1)S(1)}, bf16[4,32,1040]{2,1,0:T(8,128)(2,1)S(1)}, u32[]{:S(2)}, u32[]{:S(2)}) collective-permute-start(bf16[4,32,1040]{2,1,0:T(8,128)(2,1)S(1)} %get-tuple-element.40.refs_4_), channel_id=1, source_target_pairs={{0,8},{8,0},{1,9},{9,1},{2,10},{10,2},{3,11},{11,3},{4,12},{12,4},... | collective-permute-start | bytes 798728 | tf_op jit(solution)/shard_map/ppermute | solution.py:39
  32.2 18.7 %collective-permute-start.7 = (bf16[4,32,1040]{2,1,0:T(8,128)(2,1)S(1)}, bf16[4,32,1040]{2,1,0:T(8,128)(2,1)S(1)}, u32[]{:S(2)}, u32[]{:S(2)}) collective-permute-start(bf16[4,32,1040]{2,1,0:T(8,128)(2,1)S(1)} %get-tuple-element.40.refs_4_), channel_id=1, source_target_pairs={{0,1},{1,0},{2,3},{3,2},{4,5},{5,4},{6,7},{7,6},{8,9},{9,8},{10,11... | collective-permute-start | bytes 798728 | tf_op jit(solution)/shard_map/ppermute | solution.py:35
  32.8 13.4 %copy-start.2 = (bf16[1,256,1,8320]{3,2,1,0:T(2,128)(2,1)S(1)}, bf16[1,256,1,8320]{3,2,1,0:T(2,128)(2,1)}, u32[]{:S(2)}) copy-start(bf16[1,256,1,8320]{3,2,1,0:T(2,128)(2,1)} %get-tuple-element.36) | copy-start | bytes 12779524
  44.2 6.8 %collective-permute-start.6 = (bf16[4,32,1040]{2,1,0:T(8,128)(2,1)S(1)}, bf16[4,32,1040]{2,1,0:T(8,128)(2,1)S(1)}, u32[]{:S(2)}, u32[]{:S(2)}) collective-permute-start(bf16[4,32,1040]{2,1,0:T(8,128)(2,1)S(1)} %collective-permute-done.3.refs_1_), channel_id=1, source_target_pairs={{0,8},{8,0},{1,9},{9,1},{2,10},{10,2},{3,11},{11,3},{4,12},{12,4},... | collective-permute-start | bytes 798728 | tf_op jit(solution)/shard_map/ppermute | solution.py:39
  45.7 6.7 %collective-permute-start.8 = (bf16[4,32,1040]{2,1,0:T(8,128)(2,1)S(1)}, bf16[4,32,1040]{2,1,0:T(8,128)(2,1)S(1)}, u32[]{:S(2)}, u32[]{:S(2)}) collective-permute-start(bf16[4,32,1040]{2,1,0:T(8,128)(2,1)S(1)} %collective-permute-done.4.refs_6_), channel_id=1, source_target_pairs={{0,1},{1,0},{2,3},{3,2},{4,5},{5,4},{6,7},{7,6},{8,9},{9,8},{10,11... | collective-permute-start | bytes 798728 | tf_op jit(solution)/shard_map/ppermute | solution.py:35
  46.2 6.2 %copy-start.1 = (f32[1,8320]{1,0:T(1,128)S(1)}, f32[1,8320]{1,0:T(1,128)}, u32[]{:S(2)}) copy-start(f32[1,8320]{1,0:T(1,128)} %refs_9_.1) | copy-start | bytes 99844
  73.0 16.3 %collective-permute-start.10 = (bf16[4,2,32,1040]{3,2,1,0:T(8,128)(2,1)S(1)}, bf16[4,2,32,1040]{3,2,1,0:T(8,128)(2,1)S(1)}, u32[]{:S(2)}, u32[]{:S(2)}) collective-permute-start(bf16[4,2,32,1040]{3,2,1,0:T(8,128)(2,1)S(1)} %get-tuple-element.24), channel_id=1, source_target_pairs={{0,1},{1,0},{2,3},{3,2},{4,5},{5,4},{6,7},{7,6},{8,9},{9,8},{10,11... | collective-permute-start | bytes 1597448 | tf_op jit(solution)/shard_map/ppermute | solution.py:35
  80.8 16.8 %collective-permute-start.9 = (bf16[4,2,32,1040]{3,2,1,0:T(8,128)(2,1)S(1)}, bf16[4,2,32,1040]{3,2,1,0:T(8,128)(2,1)S(1)}, u32[]{:S(2)}, u32[]{:S(2)}) collective-permute-start(bf16[4,2,32,1040]{3,2,1,0:T(8,128)(2,1)S(1)} %get-tuple-element.22), channel_id=1, source_target_pairs={{0,1},{1,0},{2,3},{3,2},{4,5},{5,4},{6,7},{7,6},{8,9},{9,8},{10,11... | collective-permute-start | bytes 1597448 | tf_op jit(solution)/shard_map/ppermute | solution.py:35
  89.5 9.9 %collective-permute-start.11 = (bf16[4,2,32,1040]{3,2,1,0:T(8,128)(2,1)S(1)}, bf16[4,2,32,1040]{3,2,1,0:T(8,128)(2,1)S(1)}, u32[]{:S(2)}, u32[]{:S(2)}) collective-permute-start(bf16[4,2,32,1040]{3,2,1,0:T(8,128)(2,1)S(1)} %add_convert_fusion.1), channel_id=1, source_target_pairs={{0,8},{8,0},{1,9},{9,1},{2,10},{10,2},{3,11},{11,3},{4,12},{12,4},... | collective-permute-start | bytes 1597448 | tf_op jit(solution)/shard_map/ppermute | solution.py:39
  99.7 5.2 %collective-permute-start.12 = (bf16[2,32,1040]{2,1,0:T(8,128)(2,1)S(1)}, bf16[2,32,1040]{2,1,0:T(8,128)(2,1)S(1)}, u32[]{:S(2)}, u32[]{:S(2)}) collective-permute-start(bf16[2,32,1040]{2,1,0:T(8,128)(2,1)S(1)} %get-tuple-element.37), channel_id=1, source_target_pairs={{0,6},{1,7},{2,0},{3,1},{4,2},{5,3},{6,4},{7,5},{8,14},{9,15},{10,... | collective-permute-start | bytes 399368 | tf_op jit(solution)/shard_map/ppermute | solution.py:45
  100.2 9.5 %collective-permute-start.13 = (bf16[2,32,1040]{2,1,0:T(8,128)(2,1)S(1)}, bf16[2,32,1040]{2,1,0:T(8,128)(2,1)S(1)}, u32[]{:S(2)}, u32[]{:S(2)}) collective-permute-start(bf16[2,32,1040]{2,1,0:T(8,128)(2,1)S(1)} %get-tuple-element.39), channel_id=1, source_target_pairs={{0,4},{1,5},{2,6},{3,7},{4,0},{5,1},{6,2},{7,3},{8,12},{9,13},{10,... | collective-permute-start | bytes 399368 | tf_op jit(solution)/shard_map/ppermute | solution.py:45
  101.9 7.9 %collective-permute-start.14 = (bf16[2,32,1040]{2,1,0:T(8,128)(2,1)S(1)}, bf16[2,32,1040]{2,1,0:T(8,128)(2,1)S(1)}, u32[]{:S(2)}, u32[]{:S(2)}) collective-permute-start(bf16[2,32,1040]{2,1,0:T(8,128)(2,1)S(1)} %get-tuple-element.38), channel_id=1, source_target_pairs={{0,2},{1,3},{2,4},{3,5},{4,6},{5,7},{6,0},{7,1},{8,10},{9,11},{10,... | collective-permute-start | bytes 399368 | tf_op jit(solution)/shard_map/ppermute | solution.py:45
  109.8 1.4 %collective-permute-start.15 = (bf16[2,32,1040]{2,1,0:T(8,128)(2,1)S(1)}, bf16[2,32,1040]{2,1,0:T(8,128)(2,1)S(1)}, u32[]{:S(2)}, u32[]{:S(2)}) collective-permute-start(bf16[2,32,1040]{2,1,0:T(8,128)(2,1)S(1)} %get-tuple-element.31), channel_id=1, source_target_pairs={{0,16},{16,0},{1,17},{17,1},{2,18},{18,2},{3,19},{19,3},{4,20},{20... | collective-permute-start | bytes 399368 | tf_op jit(solution)/shard_map/ppermute | solution.py:316
